TPU v7x, 32 devices: a whole 2x2x4 slice. The times are simulated.
32 devices in a mesh: seq: 16 (over z, y, core), head: 2 (over x).
Axes of the slice: x: 2, y: 2, z: 4, core: 2. Of those that a mesh axis runs over, the one named last changes fastest.
Arguments:
- target: bfloat16 [4096, 2048], P('seq', 'head'), may hold values from -1000 to 1000, as said below
- source: bfloat16 [4096, 2048], P('seq', 'head'), may hold values from -6 to 6
- w_query: bfloat16 [2048, 2048], P('seq', 'head'), may hold values from -0.125 to 0.125
- w_key: bfloat16 [2048, 2048], P('seq', 'head'), may hold values from -0.125 to 0.125
- w_value: bfloat16 [2048, 2048], P('seq', 'head'), may hold values from -0.125 to 0.125
- w_out: bfloat16 [2048, 2048], P('seq', 'head'), may hold values from -0.125 to 0.125
- band_start: int32 [64], P('seq'), may hold values from 0 to 63, as said below
- band_end: int32 [64], P('seq'), may hold values from 1 to 64, as said below
- cotangent: bfloat16 [4096, 2048], P('seq', 'head'), may hold values from -6 to 6
Outputs:
- attended: bfloat16 [4096, 2048], P('seq', 'head')
- grad_target: bfloat16 [4096, 2048], P('seq', 'head')
- grad_source: bfloat16 [4096, 2048], P('seq', 'head')
Inputs may be any that keep to these rules, and one draw needn't show every extreme that they name: `target`: activations of order one, at most some rows much larger. band_start and band_end never fall from block to block; band_start[b] >= b - 1, band_start[b] < band_end[b] <= band_start[b] + 3, band_end[b] <= b + 3; some target block has a band of exactly 3 source blocks. `band_end`: see band_start.
All inputs are finite; a program needn't handle non-finite values.
Results may differ from a plain program's by a relative error of at most 0.02.
Values may be sent and summed in bfloat16 or wider, within the bound.
A program may use at most 64 MiB of HBM per device.

v0:
```python
import jax
import jax.numpy as jnp
from jax import lax
from jax.sharding import PartitionSpec as P

HEAD_DIM = 128
BLOCK = 64
MAXW = 3


def passed_along(shard, axis, by):
    count = lax.axis_size(axis)
    pairs = [(i, i + by) for i in range(count) if 0 <= i + by < count]
    return lax.ppermute(shard, axis, pairs)


def fold_rows(weight, piece):
    return jnp.dot(piece, weight, preferred_element_type=jnp.float32)


def times_transpose(left, right):
    return lax.dot_general(
        left, right, (((1,), (1,)), ((), ())), preferred_element_type=jnp.float32
    )


def per_device(target, source, w_query, w_key, w_value, w_out, band_start, band_end, cotangent):
    fone = jnp.float32
    half = jnp.bfloat16
    rows = target.shape[0]
    width = w_query.shape[1]
    heads = width // HEAD_DIM
    blocks = rows // BLOCK
    right_rows = (MAXW - 1) * BLOCK
    scale = HEAD_DIM ** (-0.5)
    wq, wk, wv, wo = (
        lax.all_gather(w_query, "seq", axis=0, tiled=True),
        lax.all_gather(w_key, "seq", axis=0, tiled=True),
        lax.all_gather(w_value, "seq", axis=0, tiled=True),
        lax.all_gather(w_out, "seq", axis=0, tiled=True),
    )
    query = fold_rows(wq, lax.all_gather(target, "head", axis=1, tiled=True)).astype(half)
    piece = lax.all_gather(source, "head", axis=1, tiled=True)
    key_sum = fold_rows(wk, piece)
    value_sum = fold_rows(wv, piece)
    packed = jnp.concatenate([key_sum.astype(half), value_sum.astype(half)], 1)
    from_prev = passed_along(packed[rows - BLOCK :], "seq", 1)
    from_next = passed_along(packed[:right_rows], "seq", -1)
    window = jnp.concatenate([from_prev, packed, from_next], 0)
    span_all = window.shape[0]
    anchor = lax.axis_index("seq") * blocks - 1
    low = band_start - anchor
    high = band_end - anchor
    count = 1
    q_blocks = query.reshape(1, rows, heads, HEAD_DIM)
    kv_blocks = window.reshape(1, span_all, 2 * heads, HEAD_DIM)
    key_block = (jnp.arange(span_all, dtype=jnp.int32) // BLOCK)[None, :]
    low_rows = jnp.repeat(low, BLOCK)[None, :]
    high_rows = jnp.repeat(high, BLOCK)[None, :]
    k_blocks = kv_blocks[:, :, :heads]
    v_blocks = kv_blocks[:, :, heads:]
    visible = (key_block[:, None, :] >= low_rows[:, :, None]) & (
        key_block[:, None, :] < high_rows[:, :, None]
    )
    scores = jnp.einsum("nqhe,nkhe->nhqk", q_blocks, k_blocks, preferred_element_type=fone) * scale
    scores = jnp.where(visible[:, None], scores, -jnp.inf)
    top = jnp.max(scores, axis=-1, keepdims=True)
    expo = jnp.exp(scores - top)
    prob = expo / jnp.sum(expo, axis=-1, keepdims=True)
    prob_b = prob.astype(half)
    context = jnp.einsum("nhqk,nkhe->nqhe", prob_b, v_blocks, preferred_element_type=fone).astype(
        half
    )
    context_flat = context.reshape(rows, width)
    attended = (
        lax.psum_scatter(
            times_transpose(context_flat, wo).astype(jnp.bfloat16),
            "head",
            scatter_dimension=1,
            tiled=True,
        )
        .astype(jnp.float32)
        .astype(half)
    )
    d_context = fold_rows(wo, lax.all_gather(cotangent, "head", axis=1, tiled=True)).astype(half)
    dc_blocks = d_context.reshape(context.shape)
    delta = jnp.sum(dc_blocks.astype(fone) * context.astype(fone), axis=-1)
    delta = jnp.transpose(delta, (0, 2, 1))[..., None]
    d_prob = jnp.einsum("nqhe,nkhe->nhqk", dc_blocks, v_blocks, preferred_element_type=fone)
    d_score = (prob * (d_prob - delta) * scale).astype(half)
    d_query = jnp.einsum("nhqk,nkhe->nqhe", d_score, k_blocks, preferred_element_type=fone).astype(
        half
    )
    dk_blocks = jnp.einsum("nhqk,nqhe->nkhe", d_score, q_blocks, preferred_element_type=fone)
    dv_blocks = jnp.einsum("nhqk,nqhe->nkhe", prob_b, dc_blocks, preferred_element_type=fone)
    dkv_blocks = jnp.concatenate(
        [dk_blocks.reshape(count, span_all, width), dv_blocks.reshape(count, span_all, width)], 2
    )
    dkv_window = dkv_blocks.reshape(span_all, 2 * width)
    back_next = passed_along(dkv_window[:BLOCK], "seq", -1)
    back_prev = passed_along(dkv_window[BLOCK + rows :], "seq", 1)
    owned = dkv_window[BLOCK : BLOCK + rows]
    owned = owned.at[rows - BLOCK :].add(back_next)
    owned = owned.at[:right_rows].add(back_prev)
    d_key = owned[:, :width].astype(half)
    d_value = owned[:, width:].astype(half)
    d_query_flat = d_query.reshape(rows, width)
    grad_target = (
        lax.psum_scatter(
            times_transpose(d_query_flat, wq).astype(jnp.bfloat16),
            "head",
            scatter_dimension=1,
            tiled=True,
        )
        .astype(jnp.float32)
        .astype(half)
    )
    source_term = times_transpose(d_key, wk) + times_transpose(d_value, wv)
    grad_source = (
        lax.psum_scatter(source_term.astype(jnp.bfloat16), "head", scatter_dimension=1, tiled=True)
        .astype(jnp.float32)
        .astype(half)
    )
    return (attended, grad_target, grad_source)


def solution(mesh):
    in_specs = (
        P("seq", "head"),
        P("seq", "head"),
        P("seq", "head"),
        P("seq", "head"),
        P("seq", "head"),
        P("seq", "head"),
        P("seq"),
        P("seq"),
        P("seq", "head"),
    )
    out_specs = (P("seq", "head"), P("seq", "head"), P("seq", "head"))
    return jax.shard_map(
        per_device, mesh=mesh, in_specs=in_specs, out_specs=out_specs, check_vma=False
    )
```

profile of v0, /device:TPU:4, one launch (start us, length us, event | category | flops | bytes accessed | tf_op | source)
XLA Modules:
  0.0 370.1 jit_solution(1944904251761183976)
XLA Ops:
  7.2 0.7 all-gather.8.cloned.1.call-update
  7.9 0.7 all-gather.12.cloned.1.call-update
  8.7 0.7 all-gather.10.cloned.1.call-update
  10.0 0.5 all-gather.18.cloned.1.call-update
  11.2 0.7 all-gather.16.cloned.1.call-update
  11.9 0.7 broadcast_subtract_fusion
  13.1 19.0 %all-gather.8.cloned.1.call-done = bf16[256,2048]{1,0:T(8,128)(2,1)} async-done(((bf16[256,1024]{1,0:T(8,128)(2,1)}), bf16[256,2048]{1,0:T(8,128)(2,1)}) %all-gather.8.cloned.1.call-update) | async-done | bytes 1048592 | tf_op jit(solution)/shard_map/all_gather | solution.py:43
  32.1 51.8 %all-gather.12.cloned.1.call-done = bf16[2048,1024]{1,0:T(8,128)(2,1)} async-done(((bf16[128,1024]{1,0:T(8,128)(2,1)}), bf16[2048,1024]{1,0:T(8,128)(2,1)}) %all-gather.12.cloned.1.call-update) | async-done | bytes 4194320 | tf_op jit(solution)/shard_map/all_gather | solution.py:39
  83.9 3.8 %convolution_convert_fusion.6 = bf16[256,1024]{1,0:T(8,128)(2,1)S(1)} fusion(bf16[256,2048]{1,0:T(8,128)(2,1)} %all-gather.8.cloned.1.call-done, bf16[2048,1024]{1,0:T(8,128)(2,1)} %all-gather.12.cloned.1.call-done), kind=kOutput, calls=%fused_computation.27 | convolution fusion | flops 1074003968 | bytes 5767168 | tf_op jit(solution)/shard_map/dot_general | solution.py:18
  87.7 47.5 %all-gather.10.cloned.1.call-done = bf16[2048,1024]{1,0:T(8,128)(2,1)} async-done(((bf16[128,1024]{1,0:T(8,128)(2,1)}), bf16[2048,1024]{1,0:T(8,128)(2,1)}) %all-gather.10.cloned.1.call-update) | async-done | bytes 4194320 | tf_op jit(solution)/shard_map/all_gather | solution.py:38
  135.2 3.4 convolution_convert_fusion.7
  138.6 0.8 pad_maximum_fusion.1
  139.5 3.2 collective-permute-start.1
  142.7 0.7 pad_maximum_fusion.2
  143.4 1.9 collective-permute-start
  145.3 12.0 %all-gather.20.cloned.1.call-done = bf16[256,2048]{1,0:T(8,128)(2,1)} async-done(((bf16[256,1024]{1,0:T(8,128)(2,1)}), bf16[256,2048]{1,0:T(8,128)(2,1)}) %all-gather.20.cloned.1.call-update) | async-done | bytes 1048592 | tf_op jit(solution)/shard_map/all_gather | solution.py:85
  157.3 51.8 %all-gather.18.cloned.1.call-done = bf16[2048,1024]{1,0:T(8,128)(2,1)} async-done(((bf16[128,1024]{1,0:T(8,128)(2,1)}), bf16[2048,1024]{1,0:T(8,128)(2,1)}) %all-gather.18.cloned.1.call-update) | async-done | bytes 4194320 | tf_op jit(solution)/shard_map/all_gather | solution.py:40
  209.2 3.8 %convolution_convert_fusion.4 = bf16[256,1024]{1,0:T(8,128)(2,1)S(1)} fusion(bf16[256,2048]{1,0:T(8,128)(2,1)} %all-gather.20.cloned.1.call-done, bf16[2048,1024]{1,0:T(8,128)(2,1)} %all-gather.18.cloned.1.call-done), kind=kOutput, calls=%fused_computation.25 | convolution fusion | flops 1074003968 | bytes 5767168 | tf_op jit(solution)/shard_map/dot_general | solution.py:18
  213.1 18.2 %all-gather.14.cloned.1.call-done = bf16[256,2048]{1,0:T(8,128)(2,1)} async-done(((bf16[256,1024]{1,0:T(8,128)(2,1)}), bf16[256,2048]{1,0:T(8,128)(2,1)}) %all-gather.14.cloned.1.call-update) | async-done | bytes 1048592 | tf_op jit(solution)/shard_map/all_gather | solution.py:42
  231.3 51.8 %all-gather.16.cloned.1.call-done = bf16[2048,1024]{1,0:T(8,128)(2,1)} async-done(((bf16[128,1024]{1,0:T(8,128)(2,1)}), bf16[2048,1024]{1,0:T(8,128)(2,1)}) %all-gather.16.cloned.1.call-update) | async-done | bytes 4194320 | tf_op jit(solution)/shard_map/all_gather | solution.py:37
  283.2 3.8 %fusion.7 = bf16[32,8,8,128]{3,2,1,0:T(8,128)(2,1)S(1)} fusion(bf16[256,2048]{1,0:T(8,128)(2,1)} %all-gather.14.cloned.1.call-done, bf16[2048,1024]{1,0:T(8,128)(2,1)} %all-gather.16.cloned.1.call-done), kind=kOutput, calls=%fused_computation.29 | convolution fusion | flops 1074003968 | bytes 5767168 | tf_op jit(solution)/shard_map/dot_general | solution.py:18
  286.9 1.2 maximum_bitcast_fusion
  288.8 0.6 fusion.9
  289.5 1.4 fusion.31
  291.2 1.4 multiply_reduce_fusion
  292.6 0.8 multiply_convert_fusion
  293.9 0.9 copy-done.7
  294.8 2.3 convolution_convert_fusion
  297.4 0.6 convolution_bitcast_fusion.1
  298.0 1.1 copy.25
  299.1 0.6 convolution_bitcast_fusion
  299.7 1.1 copy.27
  300.8 0.9 pad_maximum_fusion
  301.7 1.3 copy.73
  303.1 2.3 collective-permute-start.3
  305.3 1.0 fusion.11
  306.4 1.0 copy.74
  307.3 3.4 collective-permute-start.2
  310.8 2.4 convolution_convert_fusion.1
  313.2 3.3 slice_maximum_fusion
  316.5 0.9 copy.72
  317.7 1.4 fusion.20
  319.1 6.0 %collective-permute-done.3 = f32[128,2048]{1,0:T(8,128)S(1)} collective-permute-done((f32[128,2048]{1,0:T(8,128)}, f32[128,2048]{1,0:T(8,128)S(1)}, u32[]{:S(2)}, u32[]{:S(2)}) %collective-permute-start.3) | collective-permute-done | bytes 1048608 | tf_op jit(solution)/shard_map/ppermute | solution.py:14
  325.6 1.3 fusion.16
  326.9 1.1 copy-done.5
  328.0 2.3 fusion.2
  330.3 9.9 %reduce-scatter.4.cloned.1.call-done = bf16[256,1024]{1,0:T(8,128)(2,1)} async-done(((bf16[256,2048]{1,0:T(8,128)(2,1)}), bf16[256,1024]{1,0:T(8,128)(2,1)}) %reduce-scatter.4.cloned.1.call-update) | async-done | bytes 524304 | tf_op jit(solution)/shard_map/reduce_scatter | solution.py:76
  340.2 23.0 %reduce-scatter.8.cloned.1.call-done = bf16[256,1024]{1,0:T(8,128)(2,1)} async-done(((bf16[256,2048]{1,0:T(8,128)(2,1)}), bf16[256,1024]{1,0:T(8,128)(2,1)}) %reduce-scatter.8.cloned.1.call-update) | async-done | bytes 524304 | tf_op jit(solution)/shard_map/reduce_scatter | solution.py:120
  (48 shorter events, 4.6 us)
Async XLA Ops:
  7.2 24.9 %all-gather.8.cloned.1.call-start = ((), (), s32[]{:S(2)}) async-start(), calls=%async_computation.3 | async-start | bytes 1572864 | tf_op jit(solution)/shard_map/all_gather | solution.py:43
  7.9 76.0 %all-gather.12.cloned.1.call-start = ((), (), s32[]{:S(2)}) async-start(), calls=%async_computation.5 | async-start | bytes 4456448 | tf_op jit(solution)/shard_map/all_gather | solution.py:39
  8.6 126.5 %all-gather.10.cloned.1.call-start = ((), (), s32[]{:S(2)}) async-start(), calls=%async_computation.4 | async-start | bytes 4456448 | tf_op jit(solution)/shard_map/all_gather | solution.py:38
  9.4 147.9 %all-gather.20.cloned.1.call-start = ((), (), s32[]{:S(2)}) async-start(), calls=%async_computation.10 | async-start | bytes 1572864 | tf_op jit(solution)/shard_map/all_gather | solution.py:85
  10.0 199.2 %all-gather.18.cloned.1.call-start = ((), (), s32[]{:S(2)}) async-start(), calls=%async_computation.8 | async-start | bytes 4456448 | tf_op jit(solution)/shard_map/all_gather | solution.py:40
  10.5 220.8 %all-gather.14.cloned.1.call-start = ((), (), s32[]{:S(2)}) async-start(), calls=%async_computation.6 | async-start | bytes 1572864 | tf_op jit(solution)/shard_map/all_gather | solution.py:42
  11.1 272.0 %all-gather.16.cloned.1.call-start = ((), (), s32[]{:S(2)}) async-start(), calls=%async_computation.7 | async-start | bytes 4456448 | tf_op jit(solution)/shard_map/all_gather | solution.py:37
  11.9 318.5 %reduce-scatter.6.cloned.1.call-start = ((), (), s32[]{:S(2)}) async-start(), calls=%async_computation.11 | async-start | bytes 1572864 | tf_op jit(solution)/shard_map/reduce_scatter | solution.py:109
  32.1 103.1 %copy-start.8 = (bf16[256,2048]{1,0:T(8,128)(2,1)S(1)}, bf16[256,2048]{1,0:T(8,128)(2,1)}, u32[]{:S(2)}) copy-start(bf16[256,2048]{1,0:T(8,128)(2,1)} %all-gather.8.cloned.1.call-done) | copy-start | bytes 3145732
  139.5 147.5 %collective-permute-start.1 = (bf16[128,2048]{1,0:T(8,128)(2,1)}, bf16[128,2048]{1,0:T(8,128)(2,1)}, u32[]{:S(2)}, u32[]{:S(2)}) collective-permute-start(bf16[128,2048]{1,0:T(8,128)(2,1)} %pad_maximum_fusion.1), channel_id=1, source_target_pairs={{2,0},{4,2},{6,4},{8,6},{10,8},{12,10},{14,12},{16,14},{18,16},{20... | collective-permute-start | bytes 1572872 | tf_op jit(solution)/shard_map/ppermute | solution.py:14
  143.4 143.5 %collective-permute-start = (bf16[64,2048]{1,0:T(8,128)(2,1)}, bf16[64,2048]{1,0:T(8,128)(2,1)S(1)}, u32[]{:S(2)}, u32[]{:S(2)}) collective-permute-start(bf16[64,2048]{1,0:T(8,128)(2,1)} %pad_maximum_fusion.2), channel_id=1, source_target_pairs={{0,2},{2,4},{4,6},{6,8},{8,10},{10,12},{12,14},{14,16},{16,18},{18... | collective-permute-start | bytes 786440 | tf_op jit(solution)/shard_map/ppermute | solution.py:14
  291.2 2.2 copy-start.1
  292.6 2.2 copy-start.7
  297.1 43.1 %reduce-scatter.4.cloned.1.call-start = ((), (), s32[]{:S(2)}) async-start(), calls=%async_computation.9 | async-start | bytes 1572864 | tf_op jit(solution)/shard_map/reduce_scatter | solution.py:76
  297.3 1.7 copy-start.2
  300.8 5.6 %copy-start = (f32[1,448,8,128]{3,2,0,1:T(8,128)}, f32[1,448,8,128]{3,2,0,1:T(8,128)S(1)}, u32[]{:S(2)}) copy-start(f32[1,448,8,128]{3,2,0,1:T(8,128)S(1)} %copy.27) | copy-start | bytes 5505028
  301.7 9.0 %copy-start.3 = (bf16[8,128,256]{2,1,0:T(8,128)(2,1)S(1)}, bf16[8,128,256]{2,1,0:T(8,128)(2,1)}, u32[]{:S(2)}) copy-start(bf16[8,128,256]{2,1,0:T(8,128)(2,1)} %get-tuple-element.34) | copy-start | bytes 1572868
  301.7 9.0 %copy-start.6 = (bf16[2048,1024]{1,0:T(8,128)(2,1)S(1)}, bf16[2048,1024]{1,0:T(8,128)(2,1)}, u32[]{:S(2)}) copy-start(bf16[2048,1024]{1,0:T(8,128)(2,1)} %all-gather.18.cloned.1.call-done) | copy-start | bytes 12582916
  303.1 22.1 %collective-permute-start.3 = (f32[128,2048]{1,0:T(8,128)}, f32[128,2048]{1,0:T(8,128)S(1)}, u32[]{:S(2)}, u32[]{:S(2)}) collective-permute-start(f32[128,2048]{1,0:T(8,128)} %bitcast.91), channel_id=1, source_target_pairs={{0,2},{2,4},{4,6},{6,8},{8,10},{10,12},{12,14},{14,16},{16,18},{18... | collective-permute-start | bytes 3145736 | tf_op jit(solution)/shard_map/ppermute | solution.py:14
  307.3 10.4 %collective-permute-start.2 = (f32[64,2048]{1,0:T(8,128)}, f32[64,2048]{1,0:T(8,128)}, u32[]{:S(2)}, u32[]{:S(2)}) collective-permute-start(f32[64,2048]{1,0:T(8,128)} %bitcast.92), channel_id=1, source_target_pairs={{2,0},{4,2},{6,4},{8,6},{10,8},{12,10},{14,12},{16,14},{18,16},{20... | collective-permute-start | bytes 1572872 | tf_op jit(solution)/shard_map/ppermute | solution.py:14
  313.1 50.1 %reduce-scatter.8.cloned.1.call-start = ((), (), s32[]{:S(2)}) async-start(), calls=%async_computation.12 | async-start | bytes 1572864 | tf_op jit(solution)/shard_map/reduce_scatter | solution.py:120
  317.7 7.8 %copy-start.4 = (bf16[2048,1024]{1,0:T(8,128)(2,1)S(1)}, bf16[2048,1024]{1,0:T(8,128)(2,1)}, u32[]{:S(2)}) copy-start(bf16[2048,1024]{1,0:T(8,128)(2,1)} %all-gather.12.cloned.1.call-done) | copy-start | bytes 12582916
  325.5 2.4 copy-start.5
Sparse Core Ops, SparseCore 0:
  9.5 22.4 all-gather.7
  34.2 49.6 all-gather.11
  86.1 49.0 all-gather.9
  136.6 20.7 all-gather.19
  159.3 49.7 all-gather.17
  210.6 20.7 all-gather.13
  233.5 49.6 all-gather.15
  297.2 19.7 reduce-scatter.5
  319.9 20.2 reduce-scatter.3
  342.9 20.3 reduce-scatter.7
where the time goes:
time: 372 us; the launch traced here: 370 us
  waiting for transfers between devices  296 us (80%)
  matrix products  27.6 us (7%)
  between operations  14.5 us (4%)
  other arithmetic  12.3 us (3%)
  starting transfers between devices  11.4 us (3%)
  local copies, waits for them, and re-layouts  8.46 us (2%)
    all_gather x1, waiting for transfers between devices, per_device(): lax.all_gather(w_out, 'seq', axis=0, tiled=True)  51.8 us
    all_gather x1, waiting for transfers between devices, per_device(): lax.all_gather(w_query, 'seq', axis=0, tiled=True)  51.8 us
    all_gather x1, waiting for transfers between devices, per_device(): lax.all_gather(w_value, 'seq', axis=0, tiled=True)  51.8 us
    all_gather x1, waiting for transfers between devices, per_device(): lax.all_gather(w_key, 'seq', axis=0, tiled=True)  47.5 us
    reduce_scatter x1, waiting for transfers between devices, per_device(): lax.psum_scatter(source_term.astype(jnp.bfloat16), 'head', scatter_dimens...  23 us
    all_gather x1, waiting for transfers between devices, per_device(): piece = lax.all_gather(source, 'head', axis=1, tiled=True)  19 us
    all_gather x1, waiting for transfers between devices, per_device(): lax.all_gather(target, 'head', axis=1, tiled=True)  18.2 us
    dot_general x4, matrix products, fold_rows(): return jnp.dot(piece, weight, preferred_element_type=jnp.float32)  14.7 us
  transfers between devices with their start and end apart: 14, of which 11 were waited for; matrix products, arithmetic and copies ran while one was open for 10% of the time, Pallas kernels for 0%

commit v1 on v0

v1 whole, which is shorter than its diff:
```python
import functools

import jax
import jax.numpy as jnp
from jax import lax
from jax.experimental import pallas as pl
from jax.experimental.pallas import tpu as pltpu
from jax.sharding import PartitionSpec as P

HEAD_DIM = 128
BLOCK = 64
MAXW = 3
CHIPS_Z = 4
CORES = 2
ACT_OF = (0, 0, 1, 2)
TILE = 256


def gather_kernel(
    seqs, heads, src_ref, tgt_ref, cot_ref, wk_ref, wv_ref, wq_ref, wo_ref,
    proj_ref, wall_ref, acts, z_send, y_send, c_send, w_recv, h_send, h_recv,
):
    chips_y = seqs // (CHIPS_Z * CORES)
    me = lax.axis_index("seq")
    hm = lax.axis_index("head")
    z = me // (chips_y * CORES)
    y = lax.rem(me // CORES, chips_y)
    c = lax.rem(me, CORES)
    own = (wk_ref, wv_ref, wq_ref, wo_ref)
    depth = wk_ref.shape[0]
    rows = src_ref.shape[0]
    feats = src_ref.shape[1]
    width = wk_ref.shape[1]
    has_up = z < CHIPS_Z - 1
    has_down = z > 0

    def seq_of(zz, yy, cc):
        return (zz * chips_y + yy) * CORES + cc

    def slot(w, s):
        return wall_ref.at[w, pl.ds(pl.multiple_of(s * depth, depth), depth)]

    def send(w, s, src, sem, to):
        return pltpu.make_async_remote_copy(
            src_ref=src, dst_ref=slot(w, s), send_sem=sem, recv_sem=w_recv.at[w, s],
            device_id={"seq": to}, device_id_type=pl.DeviceIdType.MESH,
        )

    def arrived(w, s):
        send(w, s, slot(w, s), z_send.at[w, 0, 0], me).wait_recv()

    def up(w, zz, src):
        return send(w, seq_of(zz, y, c), src, z_send.at[w, zz, 0], me + chips_y * CORES)

    def down(w, zz, src):
        return send(w, seq_of(zz, y, c), src, z_send.at[w, zz, 1], me - chips_y * CORES)

    def across(w, zz, off, src):
        return send(
            w, seq_of(zz, y, c), src, y_send.at[w, zz, off],
            seq_of(z, lax.rem(y + off, chips_y), c),
        )

    def beside(w, zz, yy, src):
        return send(w, seq_of(zz, yy, c), src, c_send.at[w, zz, yy], seq_of(z, y, 1 - c))

    barrier = pltpu.get_barrier_semaphore()

    def greet(axis, to):
        pl.semaphore_signal(
            barrier, inc=1, device_id={axis: to}, device_id_type=pl.DeviceIdType.MESH
        )

    @pl.when(has_up)
    def _():
        greet("seq", me + chips_y * CORES)

    @pl.when(has_down)
    def _():
        greet("seq", me - chips_y * CORES)

    for off in range(1, chips_y):
        greet("seq", seq_of(z, lax.rem(y + off, chips_y), c))
    greet("seq", seq_of(z, y, 1 - c))
    for off in range(1, heads):
        greet("head", lax.rem(hm + off, heads))
    pl.semaphore_wait(
        barrier,
        has_up.astype(jnp.int32) + has_down.astype(jnp.int32) + chips_y - 1 + 1 + heads - 1,
    )

    def act_copy(a, off):
        ref = (src_ref, tgt_ref, cot_ref)[a]
        return pltpu.make_async_remote_copy(
            src_ref=ref, dst_ref=acts.at[a, hm], send_sem=h_send.at[a, off],
            recv_sem=h_recv.at[a, hm], device_id={"head": lax.rem(hm + off, heads)},
            device_id_type=pl.DeviceIdType.MESH,
        )

    def act_arrived(a, off):
        came = lax.rem(hm + off, heads)
        pltpu.make_async_remote_copy(
            src_ref=acts.at[a, came], dst_ref=acts.at[a, came], send_sem=h_send.at[a, off],
            recv_sem=h_recv.at[a, came], device_id={"head": came},
            device_id_type=pl.DeviceIdType.MESH,
        ).wait_recv()

    def start_own(w):
        ref = own[w]

        @pl.when(has_up)
        def _():
            up(w, z, ref).start()

        @pl.when(has_down)
        def _():
            down(w, z, ref).start()

        for off in range(1, chips_y):
            across(w, z, off, ref).start()
        beside(w, z, y, ref).start()

    def relay_z(w, d):
        low, high = z - d, z + d

        @pl.when(low >= 0)
        def _():
            s = seq_of(low, y, c)
            arrived(w, s)

            @pl.when(has_up)
            def _():
                up(w, low, slot(w, s)).start()

            for off in range(1, chips_y):
                across(w, low, off, slot(w, s)).start()
            beside(w, low, y, slot(w, s)).start()

        @pl.when(high < CHIPS_Z)
        def _():
            s = seq_of(high, y, c)
            arrived(w, s)

            @pl.when(has_down)
            def _():
                down(w, high, slot(w, s)).start()

            for off in range(1, chips_y):
                across(w, high, off, slot(w, s)).start()
            beside(w, high, y, slot(w, s)).start()

    def relay_y(w, d):
        def one(zz):
            for off in range(1, chips_y):
                yy = lax.rem(y + off, chips_y)
                s = seq_of(zz, yy, c)
                arrived(w, s)
                beside(w, zz, yy, slot(w, s)).start()

        @pl.when(z - d >= 0)
        def _():
            one(z - d)

        if d > 0:

            @pl.when(z + d < CHIPS_Z)
            def _():
                one(z + d)

    def gather(w):
        relay_z(w, 1)
        relay_y(w, 0)
        relay_z(w, 2)
        relay_y(w, 1)
        relay_z(w, 3)
        relay_y(w, 2)
        relay_y(w, 3)

    def others(w):
        def one(i, carry):
            arrived(w, i * CORES + 1 - c)
            return carry

        lax.fori_loop(0, seqs // CORES, one, 0)

    def project(w):
        tile = min(TILE, width)

        def columns(j, carry):
            cols = pl.ds(pl.multiple_of(j * tile, tile), tile)

            def part(h, total):
                return total + jnp.dot(
                    acts[ACT_OF[w], h],
                    wall_ref[w, pl.ds(pl.multiple_of(h * feats, feats), feats), cols],
                    preferred_element_type=jnp.float32,
                )

            total = lax.fori_loop(0, heads, part, jnp.zeros((rows, tile), jnp.float32))
            proj_ref[w, :, cols] = total.astype(proj_ref.dtype)
            return carry

        lax.fori_loop(0, width // tile, columns, 0)

    start_own(0)
    for off in range(1, heads):
        act_copy(0, off).start()
    start_own(1)
    for a in (1, 2):
        for off in range(1, heads):
            act_copy(a, off).start()
    for w in range(4):
        wall_ref[w, pl.ds(pl.multiple_of(me * depth, depth), depth)] = own[w][...]
    for a, ref in enumerate((src_ref, tgt_ref, cot_ref)):
        acts[a, hm] = ref[...]
    seen = set()
    for w in range(4):
        gather(w)
        if w + 2 < 4:
            start_own(w + 2)
        others(w)
        if ACT_OF[w] not in seen:
            seen.add(ACT_OF[w])
            for off in range(1, heads):
                act_arrived(ACT_OF[w], off)
        project(w)

    def drain(w):
        for zz in range(CHIPS_Z):

            @pl.when(has_up & (zz <= z))
            def _():
                up(w, zz, own[0]).wait_send()

            @pl.when(has_down & (zz >= z))
            def _():
                down(w, zz, own[0]).wait_send()

            for off in range(1, chips_y):
                across(w, zz, off, own[0]).wait_send()

            def side(yy, carry):
                beside(w, zz, yy, own[0]).wait_send()
                return carry

            lax.fori_loop(0, chips_y, side, 0)

    for w in range(4):
        drain(w)
    for a in range(3):
        for off in range(1, heads):
            act_copy(a, off).wait_send()


def gather_and_project(seqs, heads, target, source, cotangent, wk, wv, wq, wo):
    rows, feats = target.shape
    depth, width = wk.shape
    chips_y = seqs // (CHIPS_Z * CORES)
    vmem = pl.BlockSpec(memory_space=pltpu.VMEM)
    return pl.pallas_call(
        functools.partial(gather_kernel, seqs, heads),
        out_shape=(
            jax.ShapeDtypeStruct((4, rows, width), jnp.bfloat16),
            jax.ShapeDtypeStruct((4, seqs * depth, width), jnp.bfloat16),
        ),
        in_specs=[vmem] * 7,
        out_specs=(vmem, vmem),
        scratch_shapes=[
            pltpu.VMEM((3, heads, rows, feats), jnp.bfloat16),
            pltpu.SemaphoreType.DMA((4, CHIPS_Z, 2)),
            pltpu.SemaphoreType.DMA((4, CHIPS_Z, chips_y)),
            pltpu.SemaphoreType.DMA((4, CHIPS_Z, chips_y)),
            pltpu.SemaphoreType.DMA((4, seqs)),
            pltpu.SemaphoreType.DMA((3, heads)),
            pltpu.SemaphoreType.DMA((3, heads)),
        ],
        compiler_params=pltpu.CompilerParams(
            collective_id=0, has_side_effects=True, vmem_limit_bytes=48 * 1024 * 1024
        ),
        cost_estimate=pl.CostEstimate(
            flops=8 * rows * seqs * depth * width,
            bytes_accessed=8 * seqs * depth * width,
            transcendentals=0,
        ),
    )(source, target, cotangent, wk, wv, wq, wo)


def passed_along(shard, axis, by):
    count = lax.axis_size(axis)
    pairs = [(i, i + by) for i in range(count) if 0 <= i + by < count]
    return lax.ppermute(shard, axis, pairs)


def times_transpose(left, right):
    return lax.dot_general(
        left, right, (((1,), (1,)), ((), ())), preferred_element_type=jnp.float32
    )


def summed_over_heads(term):
    count = lax.axis_size("head")
    term = term.astype(jnp.bfloat16)
    if count != 2:
        return lax.psum_scatter(term, "head", scatter_dimension=1, tiled=True)
    feats = term.shape[1] // 2
    hm = lax.axis_index("head")
    away = lax.dynamic_slice_in_dim(term, (1 - hm) * feats, feats, 1)
    kept = lax.dynamic_slice_in_dim(term, hm * feats, feats, 1)
    came = lax.ppermute(away, "head", [(0, 1), (1, 0)])
    return (kept.astype(jnp.float32) + came.astype(jnp.float32)).astype(jnp.bfloat16)


def per_device(target, source, w_query, w_key, w_value, w_out, band_start, band_end, cotangent):
    fone = jnp.float32
    half = jnp.bfloat16
    rows = target.shape[0]
    width = w_query.shape[1]
    heads = width // HEAD_DIM
    blocks = rows // BLOCK
    right_rows = (MAXW - 1) * BLOCK
    scale = HEAD_DIM ** (-0.5)
    proj, wall = gather_and_project(
        lax.axis_size("seq"), lax.axis_size("head"),
        target, source, cotangent, w_key, w_value, w_query, w_out,
    )
    wk, wv, wq, wo = wall[0], wall[1], wall[2], wall[3]
    query, d_context = proj[2], proj[3]
    packed = jnp.concatenate([proj[0], proj[1]], 1)
    from_prev = passed_along(packed[rows - BLOCK :], "seq", 1)
    from_next = passed_along(packed[:right_rows], "seq", -1)
    window = jnp.concatenate([from_prev, packed, from_next], 0)
    span = window.shape[0]
    anchor = lax.axis_index("seq") * blocks - 1
    low_rows = jnp.repeat(band_start - anchor, BLOCK)[:, None]
    high_rows = jnp.repeat(band_end - anchor, BLOCK)[:, None]
    key_block = (jnp.arange(span, dtype=jnp.int32) // BLOCK)[None, :]
    visible = (key_block >= low_rows) & (key_block < high_rows)
    q = query.reshape(rows, heads, HEAD_DIM)
    dc = d_context.reshape(rows, heads, HEAD_DIM)
    kv = window.reshape(span, 2 * heads, HEAD_DIM)
    k, v = kv[:, :heads], kv[:, heads:]
    scores = jnp.einsum("qhe,khe->hqk", q, k, preferred_element_type=fone) * scale
    scores = jnp.where(visible[None], scores, -jnp.inf)
    top = jnp.max(scores, axis=-1, keepdims=True)
    expo = jnp.exp(scores - top)
    prob = expo / jnp.sum(expo, axis=-1, keepdims=True)
    prob_b = prob.astype(half)
    context = jnp.einsum("hqk,khe->qhe", prob_b, v, preferred_element_type=fone).astype(half)
    attended = summed_over_heads(times_transpose(context.reshape(rows, width), wo))
    delta = jnp.sum(dc.astype(fone) * context.astype(fone), axis=-1)
    delta = jnp.transpose(delta, (1, 0))[..., None]
    d_prob = jnp.einsum("qhe,khe->hqk", dc, v, preferred_element_type=fone)
    d_score = (prob * (d_prob - delta) * scale).astype(half)
    d_query = jnp.einsum("hqk,khe->qhe", d_score, k, preferred_element_type=fone).astype(half)
    dk = jnp.einsum("hqk,qhe->khe", d_score, q, preferred_element_type=fone)
    dv = jnp.einsum("hqk,qhe->khe", prob_b, dc, preferred_element_type=fone)
    d_window = jnp.concatenate([dk.reshape(span, width), dv.reshape(span, width)], 1)
    back_next = passed_along(d_window[:BLOCK], "seq", -1)
    back_prev = passed_along(d_window[BLOCK + rows :], "seq", 1)
    grad_target = summed_over_heads(times_transpose(d_query.reshape(rows, width), wq))
    owned = d_window[BLOCK : BLOCK + rows]
    owned = owned.at[rows - BLOCK :].add(back_next)
    owned = owned.at[:right_rows].add(back_prev)
    d_key = owned[:, :width].astype(half)
    d_value = owned[:, width:].astype(half)
    grad_source = summed_over_heads(times_transpose(d_key, wk) + times_transpose(d_value, wv))
    return (attended, grad_target, grad_source)


def solution(mesh):
    both = P("seq", "head")
    return jax.shard_map(
        per_device,
        mesh=mesh,
        in_specs=(both,) * 6 + (P("seq"), P("seq"), both),
        out_specs=(both,) * 3,
        check_vma=False,
    )
```

time: 372 us -> 191 us (0.51)
  waiting for transfers between devices: 296 us -> 27.4 us
  Pallas kernels: 0 us -> 117 us
  matrix products: 27.6 us -> 8.93 us
  between operations: 14.5 us -> 0.98 us
  local copies, waits for them, and re-layouts: 8.46 us -> 14.3 us
    all_gather x7 -> x0, waiting for transfers between devices: 252 us -> none  [the longest x1 51.8 us: per_device(): lax.all_gather(w_out, 'seq', axis=0, tiled=True)]
    pallas_call x0 -> x1, Pallas kernels: none -> 117 us  [gather_and_project(): pl.pallas_call(functools.partial(gather_kernel, seqs, heads), out_shape=(...]
    reduce_scatter x3 -> x0, waiting for transfers between devices: 32.9 us -> none  [the longest x1 23 us: per_device(): lax.psum_scatter(source_term.astype(jnp.bfloat16), 'head', scatter_dimens...]
    dot_general x10 -> x6, matrix products: 19.3 us -> 3.76 us  [the longest x1 0.78 us: per_device(): d_prob = jnp.einsum('qhe,khe->hqk', dc, v, preferred_element_type=fone)]
    ppermute x4, waiting for transfers between devices: 6.33 us -> 21.5 us  [passed_along(): return lax.ppermute(shard, axis, pairs)]
    convert_element_type x0 -> x3, other arithmetic: none -> 6.09 us  [summed_over_heads(): (kept.astype(jnp.float32) + came.astype(jnp.float32)).astype(jnp.bfloat16)]
    ppermute x0 -> x3, waiting for transfers between devices: none -> 5.95 us  [summed_over_heads(): came = lax.ppermute(away, 'head', [(0, 1), (1, 0)])]
    concatenate x4 -> x1, other arithmetic: 6.08 us -> 0.83 us  [per_device(): packed = jnp.concatenate([proj[0], proj[1]], 1)]
  transfers between devices with their start and end apart: 14 -> 7, of which waited for: 11 -> 4; matrix products, arithmetic and copies ran while one was open for 10% -> 6% of each run, Pallas kernels for 0% -> 0%
where the time goes in v1:
time: 191 us
  Pallas kernels  117 us (61%)
  waiting for transfers between devices  27.4 us (14%)
  local copies, waits for them, and re-layouts  14.3 us (7%)
  starting transfers between devices  12 us (6%)
  other arithmetic  10.2 us (5%)
  matrix products  8.93 us (5%)
    pallas_call x1, Pallas kernels, gather_and_project(): pl.pallas_call(functools.partial(gather_kernel, seqs, heads), out_shape=(...  117 us
    ppermute x4, waiting for transfers between devices, passed_along(): return lax.ppermute(shard, axis, pairs)  21.5 us
    unnamed x29, local copies, waits for them, and re-layouts  10.3 us
    ppermute x4, starting transfers between devices, passed_along(): return lax.ppermute(shard, axis, pairs)  9.47 us
    convert_element_type x3, other arithmetic, summed_over_heads(): (kept.astype(jnp.float32) + came.astype(jnp.float32)).astype(jnp.bfloat16)  6.09 us
    ppermute x3, waiting for transfers between devices, summed_over_heads(): came = lax.ppermute(away, 'head', [(0, 1), (1, 0)])  5.95 us
    dot_general x4, matrix products, times_transpose(): lax.dot_general(left, right, (((1,), (1,)), ((), ())), preferred_element_...  5.18 us
  transfers between devices with their start and end apart: 7, of which 4 were waited for; matrix products, arithmetic and copies ran while one was open for 6% of the time, Pallas kernels for 0%

profile of v1, /device:TPU:4, one launch (start us, length us, event | category | flops | bytes accessed | tf_op | source)
XLA Modules:
  0.0 190.5 jit_solution(14782381310658658950)
XLA Ops:
  0.6 1.0 copy-done
  1.7 1.0 copy-done.1
  2.7 1.0 copy-done.2
  3.8 0.9 copy-done.3
  4.7 0.9 copy-done.4
  5.7 0.9 copy-done.5
  6.6 0.9 copy-done.6
  7.6 116.7 %shard_map.112 = (bf16[4,256,1024]{2,1,0:T(8,128)(2,1)S(1)}, bf16[4,2048,1024]{2,1,0:T(8,128)(2,1)}) custom-call(bf16[256,1024]{1,0:T(8,128)(2,1)S(1)} %copy-done, bf16[256,1024]{1,0:T(8,128)(2,1)S(1)} %copy-done.1, bf16[256,1024]{1,0:T(8,128)(2,1)S(1)} %copy-done.2, bf16[128,1024]{1,0:T(8,128)(2,1)S(1)} %copy-done.3, bf16[128,1024]{1,0:T(8,128)(2,1)S(1)} %copy-done.4, ...), custom_call_target="tpu_custom_call" | custom-call | flops 4294967296 | bytes 16777216 | tf_op jit(solution)/shard_map/pallas_call | solution.py:260
  124.3 0.2 fusion.46
  124.5 0.8 pad_maximum_fusion
  125.3 3.1 %collective-permute-start.1 = (bf16[128,2048]{1,0:T(8,128)(2,1)}, bf16[128,2048]{1,0:T(8,128)(2,1)S(1)}, u32[]{:S(2)}, u32[]{:S(2)}) collective-permute-start(bf16[128,2048]{1,0:T(8,128)(2,1)} %pad_maximum_fusion), channel_id=1, source_target_pairs={{2,0},{4,2},{6,4},{8,6},{10,8},{12,10},{14,12},{16,14},{18,16},{20... | collective-permute-start | bytes 1572872 | tf_op jit(solution)/shard_map/ppermute | solution.py:291
  128.4 0.7 pad_maximum_fusion.1
  129.1 1.9 %collective-permute-start = (bf16[64,2048]{1,0:T(8,128)(2,1)}, bf16[64,2048]{1,0:T(8,128)(2,1)S(1)}, u32[]{:S(2)}, u32[]{:S(2)}) collective-permute-start(bf16[64,2048]{1,0:T(8,128)(2,1)} %pad_maximum_fusion.1), channel_id=1, source_target_pairs={{0,2},{2,4},{4,6},{6,8},{8,10},{10,12},{12,14},{14,16},{16,18},{18... | collective-permute-start | bytes 786440 | tf_op jit(solution)/shard_map/ppermute | solution.py:291
  131.1 0.2 copy.30
  131.9 9.1 %collective-permute-done = bf16[64,2048]{1,0:T(8,128)(2,1)S(1)} collective-permute-done((bf16[64,2048]{1,0:T(8,128)(2,1)}, bf16[64,2048]{1,0:T(8,128)(2,1)S(1)}, u32[]{:S(2)}, u32[]{:S(2)}) %collective-permute-start) | collective-permute-done | bytes 262176 | tf_op jit(solution)/shard_map/ppermute | solution.py:291
  141.1 0.5 copy.33
  141.8 0.6 fusion.32
  142.4 1.4 fusion.48
  143.8 0.4 fusion.29
  144.2 0.5 multiply_reduce_fusion
  144.8 0.8 multiply_convert_fusion
  145.6 0.5 convolution_convert_fusion
  146.1 0.6 convolution_bitcast_fusion.1
  146.7 0.6 convolution_bitcast_fusion
  147.4 0.2 bitcast_dynamic-update-slice_fusion.1
  147.6 0.2 bitcast_dynamic-update-slice_fusion
  147.9 0.2 slice.113
  148.3 1.4 slice-done.2
  149.6 1.2 slice-done.3
  150.8 1.3 fusion.20
  152.1 0.8 constant_dynamic-slice_fusion.2
  152.9 1.5 collective-permute-start.2
  154.4 1.9 %collective-permute-start.4 = (f32[64,2048]{1,0:T(8,128)S(1)}, f32[64,2048]{1,0:T(8,128)S(1)}, u32[]{:S(2)}, u32[]{:S(2)}) collective-permute-start(f32[64,2048]{1,0:T(8,128)S(1)} %slice.115), channel_id=1, source_target_pairs={{2,0},{4,2},{6,4},{8,6},{10,8},{12,10},{14,12},{16,14},{18,16},{20... | collective-permute-start | bytes 1572872 | tf_op jit(solution)/shard_map/ppermute | solution.py:291
  156.3 2.6 %collective-permute-start.5 = (f32[128,2048]{1,0:T(8,128)S(1)}, f32[128,2048]{1,0:T(8,128)S(1)}, u32[]{:S(2)}, u32[]{:S(2)}) collective-permute-start(f32[128,2048]{1,0:T(8,128)S(1)} %slice.117), channel_id=1, source_target_pairs={{0,2},{2,4},{4,6},{6,8},{8,10},{10,12},{12,14},{14,16},{16,18},{18... | collective-permute-start | bytes 3145736 | tf_op jit(solution)/shard_map/ppermute | solution.py:291
  158.9 1.3 fusion.23
  160.2 0.8 constant_dynamic-slice_fusion.1
  161.1 0.5 collective-permute-start.3
  161.6 1.4 collective-permute-done.4
  163.1 11.0 %collective-permute-done.5 = f32[128,2048]{1,0:T(8,128)S(1)} collective-permute-done((f32[128,2048]{1,0:T(8,128)S(1)}, f32[128,2048]{1,0:T(8,128)S(1)}, u32[]{:S(2)}, u32[]{:S(2)}) %collective-permute-start.5) | collective-permute-done | bytes 1048608 | tf_op jit(solution)/shard_map/ppermute | solution.py:291
  174.1 0.3 fusion.30
  174.5 1.3 fusion.1
  175.8 1.3 fusion.17
  177.1 0.9 constant_dynamic-slice_fusion
  177.9 0.5 collective-permute-start.6
  178.5 2.0 %add_convert_fusion.2 = bf16[256,1024]{1,0:T(8,128)(2,1)} fusion(bf16[256,1024]{1,0:T(8,128)(2,1)} %collective-permute-done.2, bf16[256,2048]{1,0:T(8,128)(2,1)S(1)} %fusion.20, s32[]{:T(128)S(6)} %select_n.27), kind=kLoop, calls=%fused_computation.38 | loop fusion | flops 1048576 | bytes 1572868 | tf_op jit(solution)/shard_map/convert_element_type | solution.py:310
  180.5 2.0 %add_convert_fusion.1 = bf16[256,1024]{1,0:T(8,128)(2,1)} fusion(bf16[256,1024]{1,0:T(8,128)(2,1)} %collective-permute-done.3, bf16[256,2048]{1,0:T(8,128)(2,1)S(1)} %fusion.23, s32[]{:T(128)S(6)} %select_n.27), kind=kLoop, calls=%fused_computation.36 | loop fusion | flops 1048576 | bytes 1572868 | tf_op jit(solution)/shard_map/convert_element_type | solution.py:310
  182.5 5.9 %collective-permute-done.6 = bf16[256,1024]{1,0:T(8,128)(2,1)} collective-permute-done((bf16[256,1024]{1,0:T(8,128)(2,1)}, bf16[256,1024]{1,0:T(8,128)(2,1)}, u32[]{:S(2)}, u32[]{:S(2)}) %collective-permute-start.6) | collective-permute-done | bytes 524320 | tf_op jit(solution)/shard_map/ppermute | solution.py:309
  188.5 2.0 %add_convert_fusion = bf16[256,1024]{1,0:T(8,128)(2,1)} fusion(bf16[256,1024]{1,0:T(8,128)(2,1)} %collective-permute-done.6, bf16[256,2048]{1,0:T(8,128)(2,1)S(1)} %fusion.17, s32[]{:T(128)S(6)} %select_n.27), kind=kLoop, calls=%fused_computation.35 | loop fusion | flops 1048576 | bytes 1572868 | tf_op jit(solution)/shard_map/convert_element_type | solution.py:310
  (35 shorter events, 1.2 us)
Async XLA Ops:
  0.6 1.0 copy-start
  1.7 1.0 copy-start.1
  2.7 1.0 copy-start.2
  3.8 0.9 copy-start.3
  4.7 0.9 copy-start.4
  5.7 0.9 copy-start.5
  6.6 0.9 copy-start.6
  124.3 6.8 %copy-start.7 = (s32[4]{0:T(128)S(1)}, s32[4]{0:T(128)}, u32[]{:S(2)}) copy-start(s32[4]{0:T(128)} %param.20) | copy-start | bytes 52
  124.3 6.8 %copy-start.8 = (s32[4]{0:T(128)S(1)}, s32[4]{0:T(128)}, u32[]{:S(2)}) copy-start(s32[4]{0:T(128)} %param.19) | copy-start | bytes 52
  125.3 15.6 %collective-permute-start.1 = (bf16[128,2048]{1,0:T(8,128)(2,1)}, bf16[128,2048]{1,0:T(8,128)(2,1)S(1)}, u32[]{:S(2)}, u32[]{:S(2)}) collective-permute-start(bf16[128,2048]{1,0:T(8,128)(2,1)} %pad_maximum_fusion), channel_id=1, source_target_pairs={{2,0},{4,2},{6,4},{8,6},{10,8},{12,10},{14,12},{16,14},{18,16},{20... | collective-permute-start | bytes 1572872 | tf_op jit(solution)/shard_map/ppermute | solution.py:291
  129.1 11.8 %collective-permute-start = (bf16[64,2048]{1,0:T(8,128)(2,1)}, bf16[64,2048]{1,0:T(8,128)(2,1)S(1)}, u32[]{:S(2)}, u32[]{:S(2)}) collective-permute-start(bf16[64,2048]{1,0:T(8,128)(2,1)} %pad_maximum_fusion.1), channel_id=1, source_target_pairs={{0,2},{2,4},{4,6},{6,8},{8,10},{10,12},{12,14},{14,16},{16,18},{18... | collective-permute-start | bytes 786440 | tf_op jit(solution)/shard_map/ppermute | solution.py:291
  144.7 3.5 %slice-start = ((s8[16777216]{0:T(1024)(128)(4,1)}), s8[4194304]{0:T(1024)(128)(4,1)S(1)}, s32[]{:S(2)}) async-start(s8[16777216]{0:T(1024)(128)(4,1)} %bitcast.67), calls=%async_computation | async-start | bytes 8388608
  144.8 3.5 %slice-start.1 = ((s8[16777216]{0:T(1024)(128)(4,1)}), s8[4194304]{0:T(1024)(128)(4,1)S(1)}, s32[]{:S(2)}) async-start(s8[16777216]{0:T(1024)(128)(4,1)} %bitcast.67), calls=%async_computation.1 | async-start | bytes 8388608
  146.1 3.5 %slice-start.2 = ((s8[16777216]{0:T(1024)(128)(4,1)}), s8[4194304]{0:T(1024)(128)(4,1)S(1)}, s32[]{:S(2)}) async-start(s8[16777216]{0:T(1024)(128)(4,1)} %bitcast.67), calls=%async_computation.2 | async-start | bytes 8388608
  147.6 3.2 %slice-start.3 = ((s8[16777216]{0:T(1024)(128)(4,1)}), s8[4194304]{0:T(1024)(128)(4,1)S(1)}, s32[]{:S(2)}) async-start(s8[16777216]{0:T(1024)(128)(4,1)} %bitcast.67), calls=%async_computation.3 | async-start | bytes 8388608
  152.9 25.5 %collective-permute-start.2 = (bf16[256,1024]{1,0:T(8,128)(2,1)}, bf16[256,1024]{1,0:T(8,128)(2,1)}, u32[]{:S(2)}, u32[]{:S(2)}) collective-permute-start(bf16[256,1024]{1,0:T(8,128)(2,1)} %constant_dynamic-slice_fusion.2), channel_id=1, source_target_pairs={{0,1},{1,0},{2,3},{3,2},{4,5},{5,4},{6,7},{7,6},{8,9},{9,8},{10,11... | collective-permute-start | bytes 1572872 | tf_op jit(solution)/shard_map/ppermute | solution.py:309
  154.4 8.6 %collective-permute-start.4 = (f32[64,2048]{1,0:T(8,128)S(1)}, f32[64,2048]{1,0:T(8,128)S(1)}, u32[]{:S(2)}, u32[]{:S(2)}) collective-permute-start(f32[64,2048]{1,0:T(8,128)S(1)} %slice.115), channel_id=1, source_target_pairs={{2,0},{4,2},{6,4},{8,6},{10,8},{12,10},{14,12},{16,14},{18,16},{20... | collective-permute-start | bytes 1572872 | tf_op jit(solution)/shard_map/ppermute | solution.py:291
  156.3 17.7 %collective-permute-start.5 = (f32[128,2048]{1,0:T(8,128)S(1)}, f32[128,2048]{1,0:T(8,128)S(1)}, u32[]{:S(2)}, u32[]{:S(2)}) collective-permute-start(f32[128,2048]{1,0:T(8,128)S(1)} %slice.117), channel_id=1, source_target_pairs={{0,2},{2,4},{4,6},{6,8},{8,10},{10,12},{12,14},{14,16},{16,18},{18... | collective-permute-start | bytes 3145736 | tf_op jit(solution)/shard_map/ppermute | solution.py:291
  161.1 19.4 %collective-permute-start.3 = (bf16[256,1024]{1,0:T(8,128)(2,1)}, bf16[256,1024]{1,0:T(8,128)(2,1)}, u32[]{:S(2)}, u32[]{:S(2)}) collective-permute-start(bf16[256,1024]{1,0:T(8,128)(2,1)} %constant_dynamic-slice_fusion.1), channel_id=1, source_target_pairs={{0,1},{1,0},{2,3},{3,2},{4,5},{5,4},{6,7},{7,6},{8,9},{9,8},{10,11... | collective-permute-start | bytes 1572872 | tf_op jit(solution)/shard_map/ppermute | solution.py:309
  177.9 10.6 %collective-permute-start.6 = (bf16[256,1024]{1,0:T(8,128)(2,1)}, bf16[256,1024]{1,0:T(8,128)(2,1)}, u32[]{:S(2)}, u32[]{:S(2)}) collective-permute-start(bf16[256,1024]{1,0:T(8,128)(2,1)} %constant_dynamic-slice_fusion), channel_id=1, source_target_pairs={{0,1},{1,0},{2,3},{3,2},{4,5},{5,4},{6,7},{7,6},{8,9},{9,8},{10,11... | collective-permute-start | bytes 1572872 | tf_op jit(solution)/shard_map/ppermute | solution.py:309

commit v2 on v1

v2 whole, which is shorter than its diff:
```python
import functools

import jax
import jax.numpy as jnp
from jax import lax
from jax.experimental import pallas as pl
from jax.experimental.pallas import tpu as pltpu
from jax.sharding import PartitionSpec as P

HEAD_DIM = 128
BLOCK = 64
MAXW = 3
CHIPS_Z = 4
CORES = 2
ACT_OF = (0, 0, 1, 2)
TILE = 256


def sublayer_kernel(
    seqs, heads, src_ref, tgt_ref, cot_ref, wk_ref, wv_ref, wq_ref, wo_ref, bias_ref,
    att_ref, gt_ref, gs_ref,
    wall_ref, acts, kvw, qd, prob_ref, probb_ref, ctx, dq, dkv, dkvb,
    edge_out_low, edge_out_high, edge_in_low, edge_in_high, outbox, inbox,
    z_send, y_send, c_send, w_recv, h_send, h_recv, own_sem,
    f_send, f_recv, b_send, b_recv, o_send, o_recv,
):
    chips_y = seqs // (CHIPS_Z * CORES)
    me = lax.axis_index("seq")
    hm = lax.axis_index("head")
    z = me // (chips_y * CORES)
    y = lax.rem(me // CORES, chips_y)
    c = lax.rem(me, CORES)
    own = (wk_ref, wv_ref, wq_ref, wo_ref)
    depth = wk_ref.shape[0]
    rows = src_ref.shape[0]
    feats = src_ref.shape[1]
    width = wk_ref.shape[1]
    has_up = z < CHIPS_Z - 1
    has_down = z > 0
    has_next = me < seqs - 1
    has_prev = me > 0
    span = kvw.shape[1]
    right = (MAXW - 1) * BLOCK
    local_heads = width // HEAD_DIM
    scale = HEAD_DIM ** (-0.5)
    layer = seqs * depth // CHIPS_Z
    piece_cols = outbox.shape[3]
    pieces = outbox.shape[1]
    subs = feats // piece_cols
    per_layer = layer // piece_cols
    outs = (att_ref, gt_ref, gs_ref)
    far = me + 2 * c - 1
    has_far = (far >= 0) & (far < seqs)

    def seq_of(zz, yy, cc):
        return (zz * chips_y + yy) * CORES + cc

    def slot(w, s):
        return wall_ref.at[w, pl.ds(pl.multiple_of(s * depth, depth), depth)]

    def send(w, s, src, sem, to):
        return pltpu.make_async_remote_copy(
            src_ref=src, dst_ref=slot(w, s), send_sem=sem, recv_sem=w_recv.at[w, s],
            device_id={"seq": to}, device_id_type=pl.DeviceIdType.MESH,
        )

    def arrived(w, s):
        send(w, s, slot(w, s), z_send.at[w, 0, 0], me).wait_recv()

    def up(w, zz, src):
        return send(w, seq_of(zz, y, c), src, z_send.at[w, zz, 0], me + chips_y * CORES)

    def down(w, zz, src):
        return send(w, seq_of(zz, y, c), src, z_send.at[w, zz, 1], me - chips_y * CORES)

    def across(w, zz, off, src):
        return send(
            w, seq_of(zz, y, c), src, y_send.at[w, zz, off],
            seq_of(z, lax.rem(y + off, chips_y), c),
        )

    def beside(w, zz, yy, src):
        return send(w, seq_of(zz, yy, c), src, c_send.at[w, zz, yy], seq_of(z, y, 1 - c))

    barrier = pltpu.get_barrier_semaphore()

    def greet(axis, to):
        pl.semaphore_signal(
            barrier, inc=1, device_id={axis: to}, device_id_type=pl.DeviceIdType.MESH
        )

    @pl.when(has_up)
    def _():
        greet("seq", me + chips_y * CORES)

    @pl.when(has_down)
    def _():
        greet("seq", me - chips_y * CORES)

    for off in range(1, chips_y):
        greet("seq", seq_of(z, lax.rem(y + off, chips_y), c))
    greet("seq", seq_of(z, y, 1 - c))

    @pl.when(has_far)
    def _():
        greet("seq", far)

    for off in range(1, heads):
        greet("head", lax.rem(hm + off, heads))
    pl.semaphore_wait(
        barrier,
        has_up.astype(jnp.int32)
        + has_down.astype(jnp.int32)
        + has_far.astype(jnp.int32)
        + (chips_y - 1 + 1 + heads - 1),
    )

    def act_copy(a, off):
        ref = (src_ref, tgt_ref, cot_ref)[a]
        return pltpu.make_async_remote_copy(
            src_ref=ref, dst_ref=acts.at[a, hm], send_sem=h_send.at[a, off],
            recv_sem=h_recv.at[a, hm], device_id={"head": lax.rem(hm + off, heads)},
            device_id_type=pl.DeviceIdType.MESH,
        )

    def act_arrived(a, off):
        came = lax.rem(hm + off, heads)
        pltpu.make_async_remote_copy(
            src_ref=acts.at[a, came], dst_ref=acts.at[a, came], send_sem=h_send.at[a, off],
            recv_sem=h_recv.at[a, came], device_id={"head": came},
            device_id_type=pl.DeviceIdType.MESH,
        ).wait_recv()

    def start_own(w):
        ref = own[w]

        @pl.when(has_up)
        def _():
            up(w, z, ref).start()

        @pl.when(has_down)
        def _():
            down(w, z, ref).start()

        for off in range(1, chips_y):
            across(w, z, off, ref).start()
        beside(w, z, y, ref).start()

    def relay_z(w, d):
        low, high = z - d, z + d

        @pl.when(low >= 0)
        def _():
            s = seq_of(low, y, c)
            arrived(w, s)

            @pl.when(has_up)
            def _():
                up(w, low, slot(w, s)).start()

            for off in range(1, chips_y):
                across(w, low, off, slot(w, s)).start()
            beside(w, low, y, slot(w, s)).start()

        @pl.when(high < CHIPS_Z)
        def _():
            s = seq_of(high, y, c)
            arrived(w, s)

            @pl.when(has_down)
            def _():
                down(w, high, slot(w, s)).start()

            for off in range(1, chips_y):
                across(w, high, off, slot(w, s)).start()
            beside(w, high, y, slot(w, s)).start()

    def relay_y(w, d):
        def one(zz):
            for off in range(1, chips_y):
                yy = lax.rem(y + off, chips_y)
                s = seq_of(zz, yy, c)
                arrived(w, s)
                beside(w, zz, yy, slot(w, s)).start()

        @pl.when(z - d >= 0)
        def _():
            one(z - d)

        if d > 0:

            @pl.when(z + d < CHIPS_Z)
            def _():
                one(z + d)

    def others(w):
        def one(i, carry):
            arrived(w, i * CORES + 1 - c)
            return carry

        lax.fori_loop(0, seqs // CORES, one, 0)

    def others_of_layer(w, zz):
        def one(yy, carry):
            arrived(w, seq_of(zz, yy, 1 - c))
            return carry

        lax.fori_loop(0, chips_y, one, 0)

    def project(w):
        tile = min(TILE, width)

        def columns(j, carry):
            cols = pl.ds(pl.multiple_of(j * tile, tile), tile)

            def part(h, total):
                return total + jnp.dot(
                    acts[ACT_OF[w], h],
                    wall_ref[w, pl.ds(pl.multiple_of(h * feats, feats), feats), cols],
                    preferred_element_type=jnp.float32,
                )

            total = lax.fori_loop(0, heads, part, jnp.zeros((rows, tile), jnp.float32))
            if w < 2:
                kvw[w, BLOCK : BLOCK + rows, cols] = total.astype(jnp.bfloat16)
            else:
                qd[w - 2, :, cols] = total.astype(jnp.bfloat16)
            return carry

        lax.fori_loop(0, width // tile, columns, 0)

    def halo_next(w):
        return pltpu.make_async_remote_copy(
            src_ref=kvw.at[w, pl.ds(rows, BLOCK)], dst_ref=kvw.at[w, pl.ds(0, BLOCK)],
            send_sem=f_send.at[w, 0], recv_sem=f_recv.at[w, 0],
            device_id={"seq": me + 1}, device_id_type=pl.DeviceIdType.MESH,
        )

    def halo_prev(w):
        return pltpu.make_async_remote_copy(
            src_ref=kvw.at[w, pl.ds(BLOCK, right)], dst_ref=kvw.at[w, pl.ds(BLOCK + rows, right)],
            send_sem=f_send.at[w, 1], recv_sem=f_recv.at[w, 1],
            device_id={"seq": me - 1}, device_id_type=pl.DeviceIdType.MESH,
        )

    def edge_next():
        return pltpu.make_async_remote_copy(
            src_ref=edge_out_high, dst_ref=edge_in_low, send_sem=b_send.at[0],
            recv_sem=b_recv.at[0], device_id={"seq": me + 1},
            device_id_type=pl.DeviceIdType.MESH,
        )

    def edge_prev():
        return pltpu.make_async_remote_copy(
            src_ref=edge_out_low, dst_ref=edge_in_high, send_sem=b_send.at[1],
            recv_sem=b_recv.at[1], device_id={"seq": me - 1},
            device_id_type=pl.DeviceIdType.MESH,
        )

    def halo_start(w):
        @pl.when(has_next)
        def _():
            halo_next(w).start()

        @pl.when(has_prev)
        def _():
            halo_prev(w).start()

    def halo_arrived():
        for w in range(2):

            @pl.when(has_prev)
            def _():
                halo_next(w).wait_recv()

            @pl.when(has_next)
            def _():
                halo_prev(w).wait_recv()

    def head_columns(h):
        return pl.ds(pl.multiple_of(h * HEAD_DIM, HEAD_DIM), HEAD_DIM)

    def dot_t(left, right_):
        return lax.dot_general(
            left, right_, (((1,), (1,)), ((), ())), preferred_element_type=jnp.float32
        )

    def dot_over_rows(left, right_):
        return lax.dot_general(
            left, right_, (((0,), (0,)), ((), ())), preferred_element_type=jnp.float32
        )

    def forward(h, carry):
        cols = head_columns(h)
        scores = dot_t(qd[0, :, cols], kvw[0, :, cols]) * scale + bias_ref[...]
        expo = jnp.exp(scores - jnp.max(scores, axis=1, keepdims=True))
        prob = expo * (1.0 / jnp.sum(expo, axis=1, keepdims=True))
        rounded = prob.astype(jnp.bfloat16)
        prob_ref[h] = prob
        probb_ref[h] = rounded
        ctx[:, cols] = jnp.dot(
            rounded, kvw[1, :, cols], preferred_element_type=jnp.float32
        ).astype(jnp.bfloat16)
        return carry

    def backward(h, carry):
        cols = head_columns(h)
        d_ctx = qd[1, :, cols]
        delta = jnp.sum(
            d_ctx.astype(jnp.float32) * ctx[:, cols].astype(jnp.float32), axis=1, keepdims=True
        )
        d_prob = dot_t(d_ctx, kvw[1, :, cols])
        d_score = (prob_ref[h] * (d_prob - delta) * scale).astype(jnp.bfloat16)
        dq[:, cols] = jnp.dot(
            d_score, kvw[0, :, cols], preferred_element_type=jnp.float32
        ).astype(jnp.bfloat16)
        dkv[0, :, cols] = dot_over_rows(d_score, qd[0, :, cols])
        dkv[1, :, cols] = dot_over_rows(probb_ref[h], d_ctx)
        return carry

    def out_copy(o, piece):
        to = piece // subs
        return pltpu.make_async_remote_copy(
            src_ref=outbox.at[o, piece], dst_ref=inbox.at[o, hm, lax.rem(piece, subs)],
            send_sem=o_send.at[o, piece], recv_sem=o_recv.at[o, hm, lax.rem(piece, subs)],
            device_id={"head": to}, device_id_type=pl.DeviceIdType.MESH,
        )

    def put_piece(o, piece):
        feat_rows = pl.ds(pl.multiple_of(piece * piece_cols, piece_cols), piece_cols)
        if o == 0:
            term = dot_t(ctx[...], wall_ref[3, feat_rows])
        elif o == 1:
            term = dot_t(dq[...], wall_ref[2, feat_rows])
        else:
            term = dot_t(dkvb[0], wall_ref[0, feat_rows]) + dot_t(dkvb[1], wall_ref[1, feat_rows])
        outbox[o, piece] = term.astype(jnp.bfloat16)

        @pl.when(piece // subs != hm)
        def _():
            out_copy(o, piece).start()

    def put_all(o):
        def one(i, carry):
            put_piece(o, lax.rem((hm + 1) * subs + i, pieces))
            return carry

        lax.fori_loop(0, pieces, one, 0)

    def finish(o):
        for sub in range(subs):
            total = outbox[o, hm * subs + sub].astype(jnp.float32)
            for off in range(1, heads):
                came = lax.rem(hm + off, heads)
                pltpu.make_async_remote_copy(
                    src_ref=inbox.at[o, came, sub], dst_ref=inbox.at[o, came, sub],
                    send_sem=o_send.at[o, 0], recv_sem=o_recv.at[o, came, sub],
                    device_id={"head": came}, device_id_type=pl.DeviceIdType.MESH,
                ).wait_recv()
                total = total + inbox[o, came, sub].astype(jnp.float32)
            outs[o][:, sub * piece_cols : (sub + 1) * piece_cols] = total.astype(jnp.bfloat16)

    def own_copy(w):
        return pltpu.make_async_copy(own[w], slot(w, me), own_sem.at[w])

    def own_act(a):
        ref = (src_ref, tgt_ref, cot_ref)[a]
        return pltpu.make_async_copy(ref, acts.at[a, hm], own_sem.at[4 + a])

    start_own(0)
    for off in range(1, heads):
        act_copy(0, off).start()
    start_own(1)
    for a in (1, 2):
        for off in range(1, heads):
            act_copy(a, off).start()
    for w in range(4):
        own_copy(w).start()
    for a in range(3):
        own_act(a).start()
    kvw[:, BLOCK + rows + right :] = jnp.zeros_like(kvw[:, BLOCK + rows + right :])

    @pl.when(me == 0)
    def _():
        kvw[:, :BLOCK] = jnp.zeros_like(kvw[:, :BLOCK])
        edge_in_low[...] = jnp.zeros_like(edge_in_low)

    @pl.when(me == seqs - 1)
    def _():
        kvw[:, BLOCK + rows : BLOCK + rows + right] = jnp.zeros_like(
            kvw[:, BLOCK + rows : BLOCK + rows + right]
        )
        edge_in_high[...] = jnp.zeros_like(edge_in_high)

    def acts_ready(a):
        own_act(a).wait()
        for off in range(1, heads):
            act_arrived(a, off)

    def complete(w, first):
        if first:
            acts_ready(ACT_OF[w])
        own_copy(w).wait()
        others(w)
        project(w)

    def attended_layer(zz):
        others_of_layer(3, zz)

        def one(j, carry):
            put_piece(0, zz * per_layer + j)
            return carry

        lax.fori_loop(0, per_layer, one, 0)

    def attended_at(d):
        @pl.when(z - d >= 0)
        def _():
            attended_layer(z - d)

        if d > 0:

            @pl.when(z + d < CHIPS_Z)
            def _():
                attended_layer(z + d)

    def gather(w, work):
        steps = [
            lambda: relay_z(w, 1), lambda: relay_y(w, 0), lambda: relay_z(w, 2),
            lambda: relay_y(w, 1), lambda: relay_z(w, 3), lambda: relay_y(w, 2),
            lambda: relay_y(w, 3),
        ]
        for i, step in enumerate(steps):
            step()
            for unit in work.get(i, ()):
                unit()

    half = local_heads // 2
    gather(0, {})
    start_own(2)
    gather(1, {0: [lambda: complete(0, True), lambda: halo_start(0)]})
    start_own(3)
    gather(2, {0: [lambda: complete(1, False), lambda: halo_start(1)]})
    gather(
        3,
        {
            0: [lambda: complete(2, True)],
            1: [halo_arrived, lambda: lax.fori_loop(0, half, forward, 0)],
            2: [lambda: lax.fori_loop(half, local_heads, forward, 0)],
            3: [lambda: own_copy(3).wait(), lambda: attended_at(0)],
            4: [lambda: attended_at(1)],
            5: [lambda: attended_at(2)],
            6: [lambda: attended_at(3)],
        },
    )
    acts_ready(2)
    project(3)
    lax.fori_loop(0, local_heads, backward, 0)
    edge_out_low[...] = dkv[:, :BLOCK].astype(jnp.bfloat16)
    edge_out_high[...] = dkv[:, BLOCK + rows : BLOCK + rows + right].astype(jnp.bfloat16)

    @pl.when(has_next)
    def _():
        edge_next().start()

    @pl.when(has_prev)
    def _():
        edge_prev().start()

    put_all(1)

    @pl.when(has_prev)
    def _():
        edge_next().wait_recv()

    @pl.when(has_next)
    def _():
        edge_prev().wait_recv()

    middle = rows - BLOCK
    dkvb[:, :right] = (
        dkv[:, BLOCK : BLOCK + right] + edge_in_low[...].astype(jnp.float32)
    ).astype(jnp.bfloat16)
    if middle > right:
        dkvb[:, right:middle] = dkv[:, BLOCK + right : BLOCK + middle].astype(jnp.bfloat16)
    dkvb[:, middle:] = (
        dkv[:, BLOCK + middle : BLOCK + rows] + edge_in_high[...].astype(jnp.float32)
    ).astype(jnp.bfloat16)
    put_all(2)
    for o in range(3):
        finish(o)

    def drain(w):
        for zz in range(CHIPS_Z):

            @pl.when(has_up & (zz <= z))
            def _():
                up(w, zz, own[0]).wait_send()

            @pl.when(has_down & (zz >= z))
            def _():
                down(w, zz, own[0]).wait_send()

            for off in range(1, chips_y):
                across(w, zz, off, own[0]).wait_send()

            def side(yy, carry):
                beside(w, zz, yy, own[0]).wait_send()
                return carry

            lax.fori_loop(0, chips_y, side, 0)

    for w in range(4):
        drain(w)
    for a in range(3):
        for off in range(1, heads):
            act_copy(a, off).wait_send()

    def out_drain(o, piece):
        @pl.when(piece // subs != hm)
        def _():
            out_copy(o, piece).wait_send()

    for o in range(3):
        for piece in range(pieces):
            out_drain(o, piece)

    @pl.when(has_next)
    def _():
        edge_next().wait_send()
        for w in range(2):
            halo_next(w).wait_send()

    @pl.when(has_prev)
    def _():
        edge_prev().wait_send()
        for w in range(2):
            halo_prev(w).wait_send()


def sublayer(seqs, heads, target, source, cotangent, wk, wv, wq, wo, bias):
    rows, feats = target.shape
    depth, width = wk.shape
    span = bias.shape[1]
    local_heads = width // HEAD_DIM
    right = (MAXW - 1) * BLOCK
    chips_y = seqs // (CHIPS_Z * CORES)
    piece_cols = min(feats, seqs * depth // CHIPS_Z)
    pieces = seqs * depth // piece_cols
    subs = feats // piece_cols
    vmem = pl.BlockSpec(memory_space=pltpu.VMEM)
    hbm = pl.BlockSpec(memory_space=pl.ANY)
    half, fone = jnp.bfloat16, jnp.float32
    return pl.pallas_call(
        functools.partial(sublayer_kernel, seqs, heads),
        out_shape=(jax.ShapeDtypeStruct((rows, feats), half),) * 3,
        in_specs=[hbm] * 7 + [vmem],
        out_specs=(vmem,) * 3,
        scratch_shapes=[
            pltpu.VMEM((4, seqs * depth, width), half),
            pltpu.VMEM((3, heads, rows, feats), half),
            pltpu.VMEM((2, span, width), half),
            pltpu.VMEM((2, rows, width), half),
            pltpu.VMEM((local_heads, rows, span), fone),
            pltpu.VMEM((local_heads, rows, span), half),
            pltpu.VMEM((rows, width), half),
            pltpu.VMEM((rows, width), half),
            pltpu.VMEM((2, span, width), fone),
            pltpu.VMEM((2, rows, width), half),
            pltpu.VMEM((2, BLOCK, width), half),
            pltpu.VMEM((2, right, width), half),
            pltpu.VMEM((2, right, width), half),
            pltpu.VMEM((2, BLOCK, width), half),
            pltpu.VMEM((3, pieces, rows, piece_cols), half),
            pltpu.VMEM((3, heads, subs, rows, piece_cols), half),
            pltpu.SemaphoreType.DMA((4, CHIPS_Z, 2)),
            pltpu.SemaphoreType.DMA((4, CHIPS_Z, chips_y)),
            pltpu.SemaphoreType.DMA((4, CHIPS_Z, chips_y)),
            pltpu.SemaphoreType.DMA((4, seqs)),
            pltpu.SemaphoreType.DMA((3, heads)),
            pltpu.SemaphoreType.DMA((3, heads)),
            pltpu.SemaphoreType.DMA((7,)),
            pltpu.SemaphoreType.DMA((2, 2)),
            pltpu.SemaphoreType.DMA((2, 2)),
            pltpu.SemaphoreType.DMA((2,)),
            pltpu.SemaphoreType.DMA((2,)),
            pltpu.SemaphoreType.DMA((3, pieces)),
            pltpu.SemaphoreType.DMA((3, heads, subs)),
        ],
        compiler_params=pltpu.CompilerParams(
            collective_id=0, has_side_effects=True, vmem_limit_bytes=56 * 1024 * 1024
        ),
        cost_estimate=pl.CostEstimate(
            flops=16 * rows * seqs * depth * width,
            bytes_accessed=8 * seqs * depth * width,
            transcendentals=local_heads * rows * span,
        ),
    )(source, target, cotangent, wk, wv, wq, wo, bias)


def per_device(target, source, w_query, w_key, w_value, w_out, band_start, band_end, cotangent):
    rows = target.shape[0]
    blocks = rows // BLOCK
    span = -(-(rows + MAXW * BLOCK) // 128) * 128
    anchor = lax.axis_index("seq") * blocks - 1
    low_rows = jnp.repeat(band_start - anchor, BLOCK)[:, None]
    high_rows = jnp.repeat(band_end - anchor, BLOCK)[:, None]
    key_block = (jnp.arange(span, dtype=jnp.int32) // BLOCK)[None, :]
    visible = (key_block >= low_rows) & (key_block < high_rows)
    bias = jnp.where(visible, 0.0, -jnp.inf).astype(jnp.float32)
    return sublayer(
        lax.axis_size("seq"), lax.axis_size("head"),
        target, source, cotangent, w_key, w_value, w_query, w_out, bias,
    )


def solution(mesh):
    both = P("seq", "head")
    return jax.shard_map(
        per_device,
        mesh=mesh,
        in_specs=(both,) * 6 + (P("seq"), P("seq"), both),
        out_specs=(both,) * 3,
        check_vma=False,
    )
```

time: 191 us -> 158 us (0.83)
  Pallas kernels: 117 us -> 151 us
  waiting for transfers between devices: 27.4 us -> 0 us
  starting transfers between devices: 12 us -> 0 us
  local copies, waits for them, and re-layouts: 14.3 us -> 4.92 us
  other arithmetic: 10.2 us -> 0.94 us
  matrix products: 8.93 us -> 0 us
    pallas_call x1, Pallas kernels: 117 us -> 151 us  [sublayer(): pl.pallas_call(functools.partial(sublayer_kernel, seqs, heads), out_shape...]
    ppermute x7 -> x0, waiting for transfers between devices: 27.4 us -> none  [the longest x4 21.5 us: passed_along(): return lax.ppermute(shard, axis, pairs)]
    ppermute x7 -> x0, starting transfers between devices: 12 us -> none  [the longest x4 9.47 us: passed_along(): return lax.ppermute(shard, axis, pairs)]
    dot_general x10 -> x0, matrix products: 8.93 us -> none  [the longest x4 5.18 us: times_transpose(): lax.dot_general(left, right, (((1,), (1,)), ((), ())), preferred_element_...]
    convert_element_type x4 -> x0, other arithmetic: 6.48 us -> none  [the longest x3 6.09 us: summed_over_heads(): (kept.astype(jnp.float32) + came.astype(jnp.float32)).astype(jnp.bfloat16)]
    unnamed x29 -> x11, local copies, waits for them, and re-layouts: 10.3 us -> 4.61 us
    dynamic_slice x3 -> x0, local copies, waits for them, and re-layouts: 2.55 us -> none  [summed_over_heads(): away = lax.dynamic_slice_in_dim(term, (1 - hm) * feats, feats, 1)]
  transfers between devices with their start and end apart: 7 -> 0, of which waited for: 4 -> 0; matrix products, arithmetic and copies ran while one was open for 6% -> 0% of each run, Pallas kernels for 0% -> 0%
where the time goes in v2:
time: 158 us
  Pallas kernels  151 us (96%)
  local copies, waits for them, and re-layouts  4.92 us (3%)
    pallas_call x1, Pallas kernels, sublayer(): pl.pallas_call(functools.partial(sublayer_kernel, seqs, heads), out_shape...  151 us
    unnamed x11, local copies, waits for them, and re-layouts  4.61 us

profile of v2, /device:TPU:4, one launch (start us, length us, event | category | flops | bytes accessed | tf_op | source)
XLA Modules:
  0.0 157.7 jit_solution(13153270296445371102)
XLA Ops:
  0.6 0.0 copy-start.2
  0.6 0.0 copy-start.3
  0.7 0.6 copy-done.2
  1.3 0.0 copy-done.3
  1.3 0.1 broadcast_in_dim.16
  1.4 0.1 lt.6
  1.5 0.1 broadcast_in_dim.15
  1.5 0.1 ge.18
  1.6 0.9 and_select_fusion.bias_ref
  2.6 151.1 %shard_map.112 = (bf16[256,1024]{1,0:T(8,128)(2,1)}, bf16[256,1024]{1,0:T(8,128)(2,1)}, bf16[256,1024]{1,0:T(8,128)(2,1)}) custom-call(bf16[256,1024]{1,0:T(8,128)(2,1)} %src_ref.1, bf16[256,1024]{1,0:T(8,128)(2,1)} %tgt_ref.1, bf16[256,1024]{1,0:T(8,128)(2,1)} %cot_ref.1, bf16[128,1024]{1,0:T(8,128)(2,1)} %wk_ref.1, bf16[128,1024]{1,0:T(8,128)(2,1)} %wv_ref.1, ...), custom_call_target="tpu_custom_call" | custom-call | flops 8589934592 | bytes 16777216 | tf_op jit(solution)/shard_map/pallas_call | solution.py:554
  153.7 0.0 copy-start.1
  153.7 1.9 %copy.15 = bf16[256,1024]{1,0:T(8,128)(2,1)} copy(bf16[256,1024]{1,0:T(8,128)(2,1)} %get-tuple-element.8) | data formatting | bytes 1048576
  155.6 0.0 copy-done.1
  155.6 0.0 copy-start
  155.6 0.8 copy.16
  156.4 0.4 copy-done
  156.9 0.8 copy.17
  (2 shorter events, 0.0 us)
Async XLA Ops:
  0.6 0.7 copy-start.2
  0.6 0.7 copy-start.3
  153.7 1.9 %copy-start.1 = (bf16[256,1024]{1,0:T(8,128)(2,1)S(1)}, bf16[256,1024]{1,0:T(8,128)(2,1)}, u32[]{:S(2)}) copy-start(bf16[256,1024]{1,0:T(8,128)(2,1)} %get-tuple-element.9) | copy-start | bytes 1572868
  155.6 1.2 copy-start

commit v3 on v2

--- a/solution.py
+++ b/solution.py
@@ -19,7 +19,7 @@
 def sublayer_kernel(
     seqs, heads, src_ref, tgt_ref, cot_ref, wk_ref, wv_ref, wq_ref, wo_ref, bias_ref,
     att_ref, gt_ref, gs_ref,
-    wall_ref, acts, kvw, qd, prob_ref, probb_ref, ctx, dq, dkv, dkvb,
+    wall_ref, acts, kvw, qd, prob_ref, probb_ref, dscore_ref, ctx, dq, dkv, dkvb,
     edge_out_low, edge_out_high, edge_in_low, edge_in_high, outbox, inbox,
     z_send, y_send, c_send, w_recv, h_send, h_recv, own_sem,
     f_send, f_recv, b_send, b_recv, o_send, o_recv,
@@ -314,8 +314,13 @@
         dq[:, cols] = jnp.dot(
             d_score, kvw[0, :, cols], preferred_element_type=jnp.float32
         ).astype(jnp.bfloat16)
-        dkv[0, :, cols] = dot_over_rows(d_score, qd[0, :, cols])
-        dkv[1, :, cols] = dot_over_rows(probb_ref[h], d_ctx)
+        dscore_ref[h] = d_score
+        return carry
+
+    def backward_source(h, carry):
+        cols = head_columns(h)
+        dkv[0, :, cols] = dot_over_rows(dscore_ref[h], qd[0, :, cols])
+        dkv[1, :, cols] = dot_over_rows(probb_ref[h], qd[1, :, cols])
         return carry
 
     def out_copy(o, piece):
@@ -340,12 +345,12 @@
         def _():
             out_copy(o, piece).start()
 
-    def put_all(o):
+    def put_pieces(o, first, last):
         def one(i, carry):
             put_piece(o, lax.rem((hm + 1) * subs + i, pieces))
             return carry
 
-        lax.fori_loop(0, pieces, one, 0)
+        lax.fori_loop(first, last, one, 0)
 
     def finish(o):
         for sub in range(subs):
@@ -370,7 +375,6 @@
     start_own(0)
     for off in range(1, heads):
         act_copy(0, off).start()
-    start_own(1)
     for a in (1, 2):
         for off in range(1, heads):
             act_copy(a, off).start()
@@ -424,38 +428,32 @@
             def _():
                 attended_layer(z + d)
 
-    def gather(w, work):
-        steps = [
-            lambda: relay_z(w, 1), lambda: relay_y(w, 0), lambda: relay_z(w, 2),
-            lambda: relay_y(w, 1), lambda: relay_z(w, 3), lambda: relay_y(w, 2),
-            lambda: relay_y(w, 3),
-        ]
-        for i, step in enumerate(steps):
-            step()
-            for unit in work.get(i, ()):
-                unit()
-
-    half = local_heads // 2
-    gather(0, {})
-    start_own(2)
-    gather(1, {0: [lambda: complete(0, True), lambda: halo_start(0)]})
-    start_own(3)
-    gather(2, {0: [lambda: complete(1, False), lambda: halo_start(1)]})
-    gather(
-        3,
-        {
-            0: [lambda: complete(2, True)],
-            1: [halo_arrived, lambda: lax.fori_loop(0, half, forward, 0)],
-            2: [lambda: lax.fori_loop(half, local_heads, forward, 0)],
-            3: [lambda: own_copy(3).wait(), lambda: attended_at(0)],
-            4: [lambda: attended_at(1)],
-            5: [lambda: attended_at(2)],
-            6: [lambda: attended_at(3)],
-        },
-    )
+    z_steps = [(w, d) for w in range(4) for d in range(1, CHIPS_Z)]
+    y_steps = [(w, d) for w in range(4) for d in range(CHIPS_Z)]
+    for i in range(len(y_steps)):
+        if i < len(z_steps):
+            w, d = z_steps[i]
+            relay_z(w, d)
+            if d == 1 and w + 1 < 4:
+                start_own(w + 1)
+        w, d = y_steps[i]
+        relay_y(w, d)
+        if w == 3:
+            if d == 0:
+                own_copy(3).wait()
+            attended_at(d)
+        elif d == CHIPS_Z - 1:
+            complete(w, ACT_OF[w] not in ACT_OF[:w])
+            if w < 2:
+                halo_start(w)
+            else:
+                halo_arrived()
+                lax.fori_loop(0, local_heads, forward, 0)
     acts_ready(2)
     project(3)
     lax.fori_loop(0, local_heads, backward, 0)
+    put_pieces(1, 0, pieces - subs)
+    lax.fori_loop(0, local_heads, backward_source, 0)
     edge_out_low[...] = dkv[:, :BLOCK].astype(jnp.bfloat16)
     edge_out_high[...] = dkv[:, BLOCK + rows : BLOCK + rows + right].astype(jnp.bfloat16)
 
@@ -467,7 +465,7 @@
     def _():
         edge_prev().start()
 
-    put_all(1)
+    put_pieces(1, pieces - subs, pieces)
 
     @pl.when(has_prev)
     def _():
@@ -486,7 +484,7 @@
     dkvb[:, middle:] = (
         dkv[:, BLOCK + middle : BLOCK + rows] + edge_in_high[...].astype(jnp.float32)
     ).astype(jnp.bfloat16)
-    put_all(2)
+    put_pieces(2, 0, pieces)
     for o in range(3):
         finish(o)
 
@@ -562,6 +560,7 @@
             pltpu.VMEM((2, span, width), half),
             pltpu.VMEM((2, rows, width), half),
             pltpu.VMEM((local_heads, rows, span), fone),
+            pltpu.VMEM((local_heads, rows, span), half),
             pltpu.VMEM((local_heads, rows, span), half),
             pltpu.VMEM((rows, width), half),
             pltpu.VMEM((rows, width), half),

time: 158 us -> 153 us (0.968); the launches traced: 158 us -> 150 us
  Pallas kernels: 151 us -> 143 us
    pallas_call x1, Pallas kernels: 151 us -> 143 us  [sublayer(): pl.pallas_call(functools.partial(sublayer_kernel, seqs, heads), out_shape...]
where the time goes in v3:
time: 153 us; the launch traced here: 150 us
  Pallas kernels  143 us (93%)
  local copies, waits for them, and re-layouts  4.92 us (3%)
    pallas_call x1, Pallas kernels, sublayer(): pl.pallas_call(functools.partial(sublayer_kernel, seqs, heads), out_shape...  143 us
    unnamed x11, local copies, waits for them, and re-layouts  4.61 us

profile of v3, /device:TPU:4, one launch (start us, length us, event | category | flops | bytes accessed | tf_op | source)
XLA Modules:
  0.0 149.6 jit_solution(12856852984999501323)
XLA Ops:
  0.6 0.0 copy-start.2
  0.6 0.0 copy-start.3
  0.7 0.6 copy-done.2
  1.3 0.0 copy-done.3
  1.3 0.1 broadcast_in_dim.16
  1.4 0.1 lt.6
  1.5 0.1 broadcast_in_dim.15
  1.5 0.1 ge.18
  1.6 0.9 and_select_fusion.bias_ref
  2.6 143.0 %shard_map.112 = (bf16[256,1024]{1,0:T(8,128)(2,1)}, bf16[256,1024]{1,0:T(8,128)(2,1)}, bf16[256,1024]{1,0:T(8,128)(2,1)}) custom-call(bf16[256,1024]{1,0:T(8,128)(2,1)} %src_ref.1, bf16[256,1024]{1,0:T(8,128)(2,1)} %tgt_ref.1, bf16[256,1024]{1,0:T(8,128)(2,1)} %cot_ref.1, bf16[128,1024]{1,0:T(8,128)(2,1)} %wk_ref.1, bf16[128,1024]{1,0:T(8,128)(2,1)} %wv_ref.1, ...), custom_call_target="tpu_custom_call" | custom-call | flops 8589934592 | bytes 16777216 | tf_op jit(solution)/shard_map/pallas_call | solution.py:552
  145.6 0.0 copy-start.1
  145.6 1.9 %copy.15 = bf16[256,1024]{1,0:T(8,128)(2,1)} copy(bf16[256,1024]{1,0:T(8,128)(2,1)} %get-tuple-element.8) | data formatting | bytes 1048576
  147.6 0.0 copy-done.1
  147.6 0.0 copy-start
  147.6 0.8 copy.16
  148.4 0.4 copy-done
  148.8 0.8 copy.17
  (2 shorter events, 0.0 us)
Async XLA Ops:
  0.6 0.7 copy-start.2
  0.6 0.7 copy-start.3
  145.6 1.9 %copy-start.1 = (bf16[256,1024]{1,0:T(8,128)(2,1)S(1)}, bf16[256,1024]{1,0:T(8,128)(2,1)}, u32[]{:S(2)}) copy-start(bf16[256,1024]{1,0:T(8,128)(2,1)} %get-tuple-element.9) | copy-start | bytes 1572868
  147.6 1.2 copy-start

commit v4 on v3

--- a/solution.py
+++ b/solution.py
@@ -16,12 +16,16 @@
 TILE = 256
 
 
+def lead_rows(depth):
+    return max(16, depth // 8)
+
+
 def sublayer_kernel(
     seqs, heads, src_ref, tgt_ref, cot_ref, wk_ref, wv_ref, wq_ref, wo_ref, bias_ref,
     att_ref, gt_ref, gs_ref,
     wall_ref, acts, kvw, qd, prob_ref, probb_ref, dscore_ref, ctx, dq, dkv, dkvb,
     edge_out_low, edge_out_high, edge_in_low, edge_in_high, outbox, inbox,
-    z_send, y_send, c_send, w_recv, h_send, h_recv, own_sem,
+    z_send, l_send, y_send, k_send, c_send, w_recv, h_send, h_recv, own_sem,
     f_send, f_recv, b_send, b_recv, o_send, o_recv,
 ):
     chips_y = seqs // (CHIPS_Z * CORES)
@@ -55,32 +59,51 @@
     def seq_of(zz, yy, cc):
         return (zz * chips_y + yy) * CORES + cc
 
+    lead = lead_rows(depth)
+    begin = (0, lead)
+    size = (lead, depth - lead)
+
     def slot(w, s):
         return wall_ref.at[w, pl.ds(pl.multiple_of(s * depth, depth), depth)]
 
-    def send(w, s, src, sem, to):
+    def part(w, s, p):
+        return wall_ref.at[w, pl.ds(pl.multiple_of(s * depth + begin[p], 16), size[p])]
+
+    def own_part(w, p):
+        return own[w].at[pl.ds(begin[p], size[p])]
+
+    def send(src, dst, send_sem, recv_sem, to):
         return pltpu.make_async_remote_copy(
-            src_ref=src, dst_ref=slot(w, s), send_sem=sem, recv_sem=w_recv.at[w, s],
+            src_ref=src, dst_ref=dst, send_sem=send_sem, recv_sem=recv_sem,
             device_id={"seq": to}, device_id_type=pl.DeviceIdType.MESH,
         )
 
-    def arrived(w, s):
-        send(w, s, slot(w, s), z_send.at[w, 0, 0], me).wait_recv()
-
-    def up(w, zz, src):
-        return send(w, seq_of(zz, y, c), src, z_send.at[w, zz, 0], me + chips_y * CORES)
-
-    def down(w, zz, src):
-        return send(w, seq_of(zz, y, c), src, z_send.at[w, zz, 1], me - chips_y * CORES)
-
-    def across(w, zz, off, src):
+    def arrived(w, s, p):
+        send(part(w, s, p), part(w, s, p), z_send.at[w, 0, 0], w_recv.at[w, s, p], me).wait_recv()
+
+    def arrived_beside(w, s):
+        send(slot(w, s), slot(w, s), z_send.at[w, 0, 0], w_recv.at[w, s, 0], me).wait_recv()
+
+    def along(w, zz, yy, p, src, step):
+        s = seq_of(zz, yy, c)
+        which = (step + 1) // 2
+        sem = z_send.at[w, zz, which] if p else l_send.at[w, zz, which, yy]
+        return send(src, part(w, s, p), sem, w_recv.at[w, s, p], me + step * chips_y * CORES)
+
+    def across(w, zz, off, p, src):
+        s = seq_of(zz, y, c)
+        sem = y_send.at[w, zz, off] if p else k_send.at[w, off]
         return send(
-            w, seq_of(zz, y, c), src, y_send.at[w, zz, off],
-            seq_of(z, lax.rem(y + off, chips_y), c),
-        )
-
-    def beside(w, zz, yy, src):
-        return send(w, seq_of(zz, yy, c), src, c_send.at[w, zz, yy], seq_of(z, y, 1 - c))
+            src, part(w, s, p), sem, w_recv.at[w, s, p], seq_of(z, lax.rem(y + off, chips_y), c)
+        )
+
+    def beside(w, zz, yy, src, dst):
+        s = seq_of(zz, yy, c)
+        return send(src, dst, c_send.at[w, zz, yy], w_recv.at[w, s, 0], seq_of(z, y, 1 - c))
+
+    def beside_part(w, zz, yy, p):
+        s = seq_of(zz, yy, c)
+        beside(w, zz, yy, part(w, s, p), part(w, s, p)).start()
 
     barrier = pltpu.get_barrier_semaphore()
 
@@ -132,56 +155,65 @@
         ).wait_recv()
 
     def start_own(w):
-        ref = own[w]
-
-        @pl.when(has_up)
-        def _():
-            up(w, z, ref).start()
-
-        @pl.when(has_down)
-        def _():
-            down(w, z, ref).start()
-
+        for p in range(2):
+            for off in range(1, chips_y):
+                across(w, z, off, p, own_part(w, p)).start()
+            onward(w, z, y, p, own_part(w, p), True, True)
+        beside(w, z, y, own[w], slot(w, me)).start()
+
+    def onward(w, zz, yy, p, src, upward, downward):
+        if upward:
+
+            @pl.when(has_up)
+            def _():
+                along(w, zz, yy, p, src, 1).start()
+
+        if downward:
+
+            @pl.when(has_down)
+            def _():
+                along(w, zz, yy, p, src, -1).start()
+
+    def relay_lead(w):
         for off in range(1, chips_y):
-            across(w, z, off, ref).start()
-        beside(w, z, y, ref).start()
+            yy = lax.rem(y + off, chips_y)
+            s = seq_of(z, yy, c)
+            arrived(w, s, 0)
+            onward(w, z, yy, 0, part(w, s, 0), True, True)
+            beside_part(w, z, yy, 0)
 
     def relay_z(w, d):
-        low, high = z - d, z + d
-
-        @pl.when(low >= 0)
-        def _():
-            s = seq_of(low, y, c)
-            arrived(w, s)
-
-            @pl.when(has_up)
-            def _():
-                up(w, low, slot(w, s)).start()
-
+        def one(zz, upward):
+            s = seq_of(zz, y, c)
+            arrived(w, s, 1)
             for off in range(1, chips_y):
-                across(w, low, off, slot(w, s)).start()
-            beside(w, low, y, slot(w, s)).start()
-
-        @pl.when(high < CHIPS_Z)
-        def _():
-            s = seq_of(high, y, c)
-            arrived(w, s)
-
-            @pl.when(has_down)
-            def _():
-                down(w, high, slot(w, s)).start()
-
-            for off in range(1, chips_y):
-                across(w, high, off, slot(w, s)).start()
-            beside(w, high, y, slot(w, s)).start()
+                across(w, zz, off, 1, part(w, s, 1)).start()
+            onward(w, zz, y, 1, part(w, s, 1), upward, not upward)
+            beside_part(w, zz, y, 1)
+
+            def ahead(yy, carry):
+                sl = seq_of(zz, yy, c)
+                arrived(w, sl, 0)
+                onward(w, zz, yy, 0, part(w, sl, 0), upward, not upward)
+                beside_part(w, zz, yy, 0)
+                return carry
+
+            lax.fori_loop(0, chips_y, ahead, 0)
+
+        @pl.when(z - d >= 0)
+        def _():
+            one(z - d, True)
+
+        @pl.when(z + d < CHIPS_Z)
+        def _():
+            one(z + d, False)
 
     def relay_y(w, d):
         def one(zz):
             for off in range(1, chips_y):
                 yy = lax.rem(y + off, chips_y)
-                s = seq_of(zz, yy, c)
-                arrived(w, s)
-                beside(w, zz, yy, slot(w, s)).start()
+                arrived(w, seq_of(zz, yy, c), 1)
+                beside_part(w, zz, yy, 1)
 
         @pl.when(z - d >= 0)
         def _():
@@ -195,14 +227,14 @@
 
     def others(w):
         def one(i, carry):
-            arrived(w, i * CORES + 1 - c)
+            arrived_beside(w, i * CORES + 1 - c)
             return carry
 
         lax.fori_loop(0, seqs // CORES, one, 0)
 
     def others_of_layer(w, zz):
         def one(yy, carry):
-            arrived(w, seq_of(zz, yy, 1 - c))
+            arrived_beside(w, seq_of(zz, yy, 1 - c))
             return carry
 
         lax.fori_loop(0, chips_y, one, 0)
@@ -213,14 +245,14 @@
         def columns(j, carry):
             cols = pl.ds(pl.multiple_of(j * tile, tile), tile)
 
-            def part(h, total):
+            def block(h, total):
                 return total + jnp.dot(
                     acts[ACT_OF[w], h],
                     wall_ref[w, pl.ds(pl.multiple_of(h * feats, feats), feats), cols],
                     preferred_element_type=jnp.float32,
                 )
 
-            total = lax.fori_loop(0, heads, part, jnp.zeros((rows, tile), jnp.float32))
+            total = lax.fori_loop(0, heads, block, jnp.zeros((rows, tile), jnp.float32))
             if w < 2:
                 kvw[w, BLOCK : BLOCK + rows, cols] = total.astype(jnp.bfloat16)
             else:
@@ -433,6 +465,8 @@
     for i in range(len(y_steps)):
         if i < len(z_steps):
             w, d = z_steps[i]
+            if d == 1:
+                relay_lead(w)
             relay_z(w, d)
             if d == 1 and w + 1 < 4:
                 start_own(w + 1)
@@ -493,20 +527,31 @@
 
             @pl.when(has_up & (zz <= z))
             def _():
-                up(w, zz, own[0]).wait_send()
+                along(w, zz, y, 1, own_part(w, 1), 1).wait_send()
 
             @pl.when(has_down & (zz >= z))
             def _():
-                down(w, zz, own[0]).wait_send()
+                along(w, zz, y, 1, own_part(w, 1), -1).wait_send()
 
             for off in range(1, chips_y):
-                across(w, zz, off, own[0]).wait_send()
+                across(w, zz, off, 1, own_part(w, 1)).wait_send()
 
             def side(yy, carry):
-                beside(w, zz, yy, own[0]).wait_send()
+                beside(w, zz, yy, own[w], slot(w, me)).wait_send()
+
+                @pl.when(has_up & (zz <= z))
+                def _():
+                    along(w, zz, yy, 0, own_part(w, 0), 1).wait_send()
+
+                @pl.when(has_down & (zz >= z))
+                def _():
+                    along(w, zz, yy, 0, own_part(w, 0), -1).wait_send()
+
                 return carry
 
             lax.fori_loop(0, chips_y, side, 0)
+        for off in range(1, chips_y):
+            across(w, z, off, 0, own_part(w, 0)).wait_send()
 
     for w in range(4):
         drain(w)
@@ -573,9 +618,11 @@
             pltpu.VMEM((3, pieces, rows, piece_cols), half),
             pltpu.VMEM((3, heads, subs, rows, piece_cols), half),
             pltpu.SemaphoreType.DMA((4, CHIPS_Z, 2)),
+            pltpu.SemaphoreType.DMA((4, CHIPS_Z, 2, chips_y)),
             pltpu.SemaphoreType.DMA((4, CHIPS_Z, chips_y)),
+            pltpu.SemaphoreType.DMA((4, chips_y)),
             pltpu.SemaphoreType.DMA((4, CHIPS_Z, chips_y)),
-            pltpu.SemaphoreType.DMA((4, seqs)),
+            pltpu.SemaphoreType.DMA((4, seqs, 2)),
             pltpu.SemaphoreType.DMA((3, heads)),
             pltpu.SemaphoreType.DMA((3, heads)),
             pltpu.SemaphoreType.DMA((7,)),

time: 153 us -> 150 us (0.980)
  the two profiles are of different devices: /device:TPU:4 before, /device:TPU:0 now
where the time goes in v4:
time: 150 us
  Pallas kernels  143 us (95%)
  local copies, waits for them, and re-layouts  4.92 us (3%)
    pallas_call x1, Pallas kernels, sublayer(): pl.pallas_call(functools.partial(sublayer_kernel, seqs, heads), out_shape...  143 us
    unnamed x11, local copies, waits for them, and re-layouts  4.61 us

profile of v4, /device:TPU:0, one launch (start us, length us, event | category | flops | bytes accessed | tf_op | source)
XLA Modules:
  0.0 150.0 jit_solution(6903247548798973803)
XLA Ops:
  0.6 0.0 copy-start.2
  0.6 0.0 copy-start.3
  0.7 0.6 copy-done.2
  1.3 0.0 copy-done.3
  1.3 0.1 broadcast_in_dim.16
  1.4 0.1 lt.6
  1.5 0.1 broadcast_in_dim.15
  1.5 0.1 ge.18
  1.6 0.9 and_select_fusion.bias_ref
  2.6 143.5 %shard_map.112 = (bf16[256,1024]{1,0:T(8,128)(2,1)}, bf16[256,1024]{1,0:T(8,128)(2,1)}, bf16[256,1024]{1,0:T(8,128)(2,1)}) custom-call(bf16[256,1024]{1,0:T(8,128)(2,1)} %src_ref.1, bf16[256,1024]{1,0:T(8,128)(2,1)} %tgt_ref.1, bf16[256,1024]{1,0:T(8,128)(2,1)} %cot_ref.1, bf16[128,1024]{1,0:T(8,128)(2,1)} %wk_ref.1, bf16[128,1024]{1,0:T(8,128)(2,1)} %wv_ref.1, ...), custom_call_target="tpu_custom_call" | custom-call | flops 8589934592 | bytes 16777216 | tf_op jit(solution)/shard_map/pallas_call | solution.py:597
  146.0 0.0 copy-start.1
  146.1 1.9 %copy.15 = bf16[256,1024]{1,0:T(8,128)(2,1)} copy(bf16[256,1024]{1,0:T(8,128)(2,1)} %get-tuple-element.8) | data formatting | bytes 1048576
  148.0 0.0 copy-done.1
  148.0 0.0 copy-start
  148.0 0.8 copy.16
  148.8 0.4 copy-done
  149.2 0.8 copy.17
  (2 shorter events, 0.0 us)
Async XLA Ops:
  0.6 0.7 copy-start.2
  0.6 0.7 copy-start.3
  146.0 1.9 %copy-start.1 = (bf16[256,1024]{1,0:T(8,128)(2,1)S(1)}, bf16[256,1024]{1,0:T(8,128)(2,1)}, u32[]{:S(2)}) copy-start(bf16[256,1024]{1,0:T(8,128)(2,1)} %get-tuple-element.9) | copy-start | bytes 1572868
  148.0 1.2 copy-start
